TPU v7x, 512 devices: a whole 4x4x16 slice. The times are simulated.
512 devices in a mesh: dp: 2 (over core), seq: 16 (over y, x), head: 16 (over z).
Axes of the slice: x: 4, y: 4, z: 16, core: 2. Of those that a mesh axis runs over, the one named last changes fastest.
Arguments:
- queries: bfloat16 [65536, 32, 128], P(('dp', 'seq', 'head')), parts along dimension 0, may hold values from -6 to 6
- keys: bfloat16 [65536, 4, 128], P(('dp', 'seq', 'head')), parts along dimension 0, may hold values from -6 to 6
- values: bfloat16 [65536, 4, 128], P(('dp', 'seq', 'head')), parts along dimension 0, may hold values from -6 to 6
- out_grad: bfloat16 [65536, 32, 128], P(('dp', 'seq', 'head')), parts along dimension 0, may hold values from -24 to 24
- kept_blocks: int32 [4, 256, 1], replicated, may hold values from 0 to 255, as said below
- sink_blocks: int32 [4], replicated, may hold values from 1 to 3
- window_blocks: int32 [4], replicated, may hold values from 2 to 4
Outputs:
- grad_queries: bfloat16 [65536, 32, 128], P(('dp', 'seq', 'head')), parts along dimension 0
- grad_keys: bfloat16 [65536, 4, 128], P(('dp', 'seq', 'head')), parts along dimension 0
- grad_values: bfloat16 [65536, 4, 128], P(('dp', 'seq', 'head')), parts along dimension 0
There are 2 independent parts, one for each index of `dp`. A program takes and returns all parts, laid end to end along the dimension named above; an argument that names none is the same for every part. Nothing has to cross between parts.
Inputs may be any that keep to these rules, and one draw needn't show every extreme that they name: `kept_blocks`: entries that name a block after the query block are ignored; entries may name sink or window blocks. For each key head and each index of seq, the 16 entries of that index's query blocks name blocks held by one index of seq at most 2 times in all, and exactly 2 times for some index of seq.
All inputs are finite; a program needn't handle non-finite values.
Results may differ from a plain program's by a relative error of at most 0.0076.
Values may be sent and summed in bfloat16 or wider, within the bound.
A program may use at most 128 MiB of HBM per device.

v0:
```python
import math

import jax
import jax.numpy as jnp
import numpy as np
from jax import lax
from jax.sharding import PartitionSpec as P

BLK = 128
SINK_MOST = 3
WIN_MOST = 4


def spread(array, axis, root):
    mine = lax.axis_index(axis) == root
    return lax.psum(jnp.where(mine, array, jnp.zeros_like(array)), axis)


def shifted(block, axis, distance):
    devices = range(lax.axis_size(axis))
    route = [(i - distance, i) for i in devices if i - distance in devices]
    return lax.ppermute(block, axis, route)


def slot_table(query_blocks, kept_rows, sink_count, window_count):
    current = query_blocks[:, None]
    number = query_blocks.shape[0]
    sink_ids = jnp.broadcast_to(
        jnp.arange(SINK_MOST, dtype=jnp.int32)[None, :], (number, SINK_MOST)
    )
    sink_ok = (sink_ids < sink_count) & (sink_ids <= current) & (current - sink_ids >= window_count)
    offsets = jnp.arange(WIN_MOST, dtype=jnp.int32)[None, :]
    window_ids = current - offsets
    window_ok = (offsets < window_count) & (window_ids >= 0)
    kept_ok = (
        (kept_rows <= current) & (kept_rows >= sink_count) & (current - kept_rows >= window_count)
    )
    repeated = jnp.zeros((number,), dtype=bool)
    fresh = [jnp.logical_not(repeated)]
    kept_ok = kept_ok & jnp.stack(fresh, axis=1)
    slot_ids = jnp.concatenate([sink_ids, window_ids, kept_rows], axis=1)
    slot_ok = jnp.concatenate([sink_ok, window_ok, kept_ok], axis=1)
    return (jnp.maximum(slot_ids, 0), slot_ok)


def slot_mask(slot_ok):
    number, slots = slot_ok.shape
    within = jnp.arange(BLK, dtype=jnp.int32)
    diagonal = within[None, :] <= within[:, None]
    on_diagonal = jnp.arange(slots, dtype=jnp.int32) == SINK_MOST
    allowed = slot_ok[:, None, :, None] & (
        jnp.logical_not(on_diagonal)[None, None, :, None] | diagonal[None, :, None, :]
    )
    return allowed.reshape(number, BLK, slots * BLK)


def body(queries, keys, values, out_grad, kept_blocks, sink_blocks, window_blocks):
    head_count = lax.axis_size("head")
    seq_count = lax.axis_size("seq")
    seq_index = lax.axis_index("seq")
    head_index = lax.axis_index("head")
    kv_total = keys.shape[1]
    repeat = head_count // kv_total
    keys_wide = jnp.repeat(keys, repeat, axis=1)
    values_wide = jnp.repeat(values, repeat, axis=1)
    q_local, k_local, v_local, grad_local = (
        lax.all_to_all(queries, "head", split_axis=1, concat_axis=0, tiled=True),
        lax.all_to_all(keys_wide, "head", split_axis=1, concat_axis=0, tiled=True),
        lax.all_to_all(values_wide, "head", split_axis=1, concat_axis=0, tiled=True),
        lax.all_to_all(out_grad, "head", split_axis=1, concat_axis=0, tiled=True),
    )
    seq_rows, heads_here, width = q_local.shape
    local_blocks = seq_rows // BLK
    scale = 1.0 / math.sqrt(width)
    kv_pairs = jnp.concatenate([k_local[:, 0], v_local[:, 0]], axis=1)
    pair_blocks = kv_pairs.reshape(local_blocks, BLK, 2 * width)
    sink_pairs = spread(kv_pairs[: SINK_MOST * BLK], "seq", 0).reshape(SINK_MOST, BLK, 2 * width)
    reach = WIN_MOST - 1
    before = shifted(kv_pairs[seq_rows - reach * BLK :], "seq", 1)
    extended = jnp.concatenate([before, kv_pairs], axis=0).reshape(
        local_blocks + reach, BLK, 2 * width
    )
    kv_head = head_index // repeat
    head_lists = lax.dynamic_index_in_dim(kept_blocks, kv_head, 0, keepdims=False)
    sink_count = lax.dynamic_index_in_dim(sink_blocks, kv_head, 0, keepdims=False)
    window_count = lax.dynamic_index_in_dim(window_blocks, kv_head, 0, keepdims=False)
    keep = head_lists.shape[1]
    entries = local_blocks * keep
    capacity = max(2, -(-entries // seq_count))
    all_lists = head_lists.reshape(seq_count, entries)
    owners = all_lists // local_blocks
    order = jnp.arange(entries, dtype=jnp.int32)
    earlier_mask = order[None, :] < order[:, None]
    ranks = jnp.sum(
        ((owners[:, :, None] == owners[:, None, :]) & earlier_mask[None]).astype(jnp.int32), axis=2
    )
    place_ids = jnp.arange(capacity, dtype=jnp.int32)
    sent_match = (owners[:, None, :] == seq_index) & (ranks[:, None, :] == place_ids[None, :, None])
    sent_block = jnp.sum(
        jnp.where(sent_match, all_lists[:, None, :] - seq_index * local_blocks, 0), axis=2
    )
    outgoing = pair_blocks[sent_block]
    incoming = lax.all_to_all(outgoing, "seq", split_axis=0, concat_axis=0, tiled=True)
    my_lists = lax.dynamic_index_in_dim(all_lists, seq_index, 0, keepdims=False)
    my_owners = my_lists // local_blocks
    my_ranks = lax.dynamic_index_in_dim(ranks, seq_index, 0, keepdims=False)
    far_pairs = incoming.reshape(seq_count * capacity, BLK, 2 * width)[
        my_owners * capacity + my_ranks
    ]
    query_blocks = seq_index * local_blocks + jnp.arange(local_blocks, dtype=jnp.int32)
    unused_ids, slot_ok = slot_table(
        query_blocks, my_lists.reshape(local_blocks, keep), sink_count, window_count
    )
    allowed = slot_mask(slot_ok)
    slots = SINK_MOST + WIN_MOST + keep
    span = 2
    turns = local_blocks // span
    window_index = np.array(
        [[row + reach - offset for offset in range(WIN_MOST)] for row in range(span)],
        dtype=np.int32,
    )

    def turn(carry, inputs):
        near_sum, sink_sum = carry
        position, q_part, g_part, mask_part, far_part = inputs
        window_part = lax.dynamic_slice_in_dim(extended, position * span, span + reach, 0)
        window_slots = window_part[window_index]
        sink_slots = jnp.broadcast_to(sink_pairs[None], (span,) + sink_pairs.shape)
        gathered = jnp.concatenate([sink_slots, window_slots, far_part], axis=1).reshape(
            span, slots * BLK, 2 * width
        )
        key_part = gathered[..., :width]
        value_part = gathered[..., width:]
        scores = (
            jnp.einsum("bthd,bud->bhtu", q_part, key_part, preferred_element_type=jnp.float32)
            * scale
        )
        scores = jnp.where(mask_part[:, None], scores, -jnp.inf)
        top = jnp.max(scores, axis=3, keepdims=True)
        lse = top + jnp.log(jnp.sum(jnp.exp(scores - top), axis=3, keepdims=True))
        probs = jnp.exp(scores - lse)
        probs_low = probs.astype(jnp.bfloat16)
        dprobs = jnp.einsum(
            "bthd,bud->bhtu", g_part, value_part, preferred_element_type=jnp.float32
        )
        delta = jnp.sum(probs * dprobs, axis=3, keepdims=True)
        dscores = (probs * (dprobs - delta)).astype(jnp.bfloat16)
        grad_q = (
            jnp.einsum("bhtu,bud->bthd", dscores, key_part, preferred_element_type=jnp.float32)
            * scale
        ).astype(jnp.bfloat16)
        key_terms = (
            jnp.einsum("bhtu,bthd->bud", dscores, q_part, preferred_element_type=jnp.float32)
            * scale
        )
        value_terms = jnp.einsum(
            "bhtu,bthd->bud", probs_low, g_part, preferred_element_type=jnp.float32
        )
        terms = jnp.concatenate([key_terms, value_terms], axis=2).reshape(
            span, slots, BLK, 2 * width
        )
        sink_sum = sink_sum + jnp.sum(terms[:, :SINK_MOST], axis=0)
        window_terms = terms[:, SINK_MOST : SINK_MOST + WIN_MOST]
        placed = (
            jnp.zeros((span + reach, BLK, 2 * width), jnp.float32)
            .at[window_index]
            .add(window_terms)
        )
        previous = lax.dynamic_slice_in_dim(near_sum, position * span, span + reach, 0)
        near_sum = lax.dynamic_update_slice_in_dim(near_sum, previous + placed, position * span, 0)
        return ((near_sum, sink_sum), (grad_q, terms[:, SINK_MOST + WIN_MOST :]))

    start = (
        jnp.zeros((local_blocks + reach, BLK, 2 * width), jnp.float32),
        jnp.zeros((SINK_MOST, BLK, 2 * width), jnp.float32),
    )
    scan_inputs = (
        jnp.arange(turns, dtype=jnp.int32),
        q_local.reshape(turns, span, BLK, heads_here, width),
        grad_local.reshape(turns, span, BLK, heads_here, width),
        allowed.reshape(turns, span, BLK, slots * BLK),
        far_pairs.reshape(turns, span, keep, BLK, 2 * width),
    )
    (near_sum, sink_sum), (grad_blocks, far_terms) = lax.scan(turn, start, scan_inputs)
    grad_rows = grad_blocks.reshape(seq_rows, heads_here, width)
    grad_queries = lax.all_to_all(grad_rows, "head", split_axis=0, concat_axis=1, tiled=True)
    far_terms = far_terms.reshape(entries, BLK, 2 * width)
    owner_ids = jnp.arange(seq_count, dtype=jnp.int32)
    back_match = (my_owners[None, None, :] == owner_ids[:, None, None]) & (
        my_ranks[None, None, :] == place_ids[None, :, None]
    )
    outbound = jnp.einsum(
        "ocp,pbd->ocbd", back_match.astype(jnp.float32), far_terms, precision=lax.Precision.HIGHEST
    )
    sent_valid = jnp.any(sent_match, axis=2)
    owner_hits = (
        (sent_block[:, :, None] == jnp.arange(local_blocks, dtype=jnp.int32)[None, None, :])
        & sent_valid[:, :, None]
    ).astype(jnp.float32)
    arrived = lax.all_to_all(outbound, "seq", split_axis=0, concat_axis=0, tiled=True)
    far_added = jnp.einsum("rcb,rctd->btd", owner_hits, arrived, precision=lax.Precision.HIGHEST)
    spill = shifted(near_sum[:reach], "seq", -1)
    sink_total = lax.psum(sink_sum, "seq")
    own = near_sum[reach:] + far_added
    own = own + jnp.concatenate(
        [jnp.zeros((local_blocks - reach, BLK, 2 * width), jnp.float32), spill], axis=0
    )
    sink_share = jnp.where(seq_index == 0, sink_total, jnp.zeros_like(sink_total))
    own = own + jnp.concatenate(
        [sink_share, jnp.zeros((local_blocks - SINK_MOST, BLK, 2 * width), jnp.float32)], axis=0
    )
    flat = own.reshape(seq_rows, 1, 2 * width)
    returned = lax.all_to_all(flat, "head", split_axis=0, concat_axis=1, tiled=True)
    tok_rows = returned.shape[0]
    combined = jnp.sum(returned.reshape(tok_rows, kv_total, repeat, 2 * width), axis=2)
    grad_keys = combined[..., :width].astype(jnp.bfloat16)
    grad_values = combined[..., width:].astype(jnp.bfloat16)
    return (grad_queries, grad_keys, grad_values)


def solution(mesh):
    placed = (
        P(("dp", "seq", "head"), None, None),
        P(("dp", "seq", "head"), None, None),
        P(("dp", "seq", "head"), None, None),
        P(("dp", "seq", "head"), None, None),
        P(),
        P(),
        P(),
    )
    return jax.shard_map(
        body,
        mesh=mesh,
        in_specs=placed,
        out_specs=(
            P(("dp", "seq", "head"), None, None),
            P(("dp", "seq", "head"), None, None),
            P(("dp", "seq", "head"), None, None),
        ),
        check_vma=False,
    )
```

profile of v0, /device:TPU:24, one launch (start us, length us, event | category | flops | bytes accessed | tf_op | source)
XLA Modules:
  0.0 893.0 jit_solution(6246537948425911620)
XLA Ops:
  9.0 15.2 %all-to-all-start = ((bf16[128,16,128]{2,0,1:T(8,128)(2,1)}), bf16[128,16,128]{2,0,1:T(8,128)(2,1)S(1)}, u32[]{:S(2)}, u32[]{:S(2)}) async-start(bf16[128,16,128]{2,0,1:T(8,128)(2,1)} %bitcast.5), calls=%async_computation | async-start | bytes 1048576 | tf_op jit(solution)/shard_map/all_to_all | solution.py:68
  25.1 28.2 %all-to-all-done = bf16[128,16,128]{2,0,1:T(8,128)(2,1)S(1)} async-done(((bf16[128,16,128]{2,0,1:T(8,128)(2,1)}), bf16[128,16,128]{2,0,1:T(8,128)(2,1)S(1)}, u32[]{:S(2)}, u32[]{:S(2)}) %all-to-all-start) | async-done | bytes 524320 | tf_op jit(solution)/shard_map/all_to_all | solution.py:68
  54.2 6.3 all-to-all-start.1
  61.4 28.2 %all-to-all-done.1 = bf16[128,16,128]{2,0,1:T(8,128)(2,1)S(1)} async-done(((bf16[128,16,128]{2,0,1:T(8,128)(2,1)}), bf16[128,16,128]{2,0,1:T(8,128)(2,1)S(1)}, u32[]{:S(2)}, u32[]{:S(2)}) %all-to-all-start.1) | async-done | bytes 524320 | tf_op jit(solution)/shard_map/all_to_all | solution.py:69
  91.8 7.3 all-to-all-start.2
  100.5 21.3 %all-to-all-done.2 = bf16[16,2,128,256]{3,2,1,0:T(8,128)(2,1)} async-done(((bf16[16,2,128,256]{3,2,1,0:T(8,128)(2,1)}), bf16[16,2,128,256]{3,2,1,0:T(8,128)(2,1)}, u32[]{:S(2)}, u32[]{:S(2)}) %all-to-all-start.2) | async-done | bytes 2097184 | tf_op jit(solution)/shard_map/all_to_all | solution.py:103
  121.8 14.1 %all-to-all-start.3 = ((bf16[128,32,128]{2,0,1:T(8,128)(2,1)}), bf16[128,32,128]{2,0,1:T(8,128)(2,1)}, u32[]{:S(2)}, u32[]{:S(2)}) async-start(bf16[128,32,128]{2,0,1:T(8,128)(2,1)} %copy.112), calls=%async_computation.3 | async-start | bytes 2097152 | tf_op jit(solution)/shard_map/all_to_all | solution.py:67
  137.3 47.3 %all-to-all-done.3 = bf16[128,32,128]{2,0,1:T(8,128)(2,1)} async-done(((bf16[128,32,128]{2,0,1:T(8,128)(2,1)}), bf16[128,32,128]{2,0,1:T(8,128)(2,1)}, u32[]{:S(2)}, u32[]{:S(2)}) %all-to-all-start.3) | async-done | bytes 1048608 | tf_op jit(solution)/shard_map/all_to_all | solution.py:67
  184.6 8.2 all-to-all-start.4
  198.8 4.7 broadcast_and_fusion
  206.9 7.8 collective-permute-done
  214.9 3.2 gather_fusion.2
  218.1 104.7 %all-reduce.5.cloned.1.call-done = bf16[384,256]{1,0:T(8,128)(2,1)} async-done(((bf16[384,256]{1,0:T(8,128)(2,1)}), bf16[384,256]{1,0:T(8,128)(2,1)}) %all-reduce.5.cloned.1.call-update) | async-done | bytes 196624 | tf_op jit(solution)/shard_map/psum | solution.py:16
  324.5 233.6 %while.19 = (s32[]{:T(128)}, f32[19,128,256]{2,1,0:T(8,128)}, f32[3,128,256]{1,0,2:T(4,128)}, bf16[8,2,128,2,128]{4,2,1,0,3:T(8,128)(2,1)}, f32[8,2,1,128,256]{3...) while((s32[]{:T(128)}, f32[19,128,256]{2,1,0:T(8,128)}, ...), condition=%wide.region_9.10_spmd.clone.clone.clone, body=%wide.region_3.9_spmd.sunk.clone.clone.clone.sunk | while | flops 680951808 | bytes 64059104 | solution.py:184
  337.0 2.5 copy.158
  341.6 3.7 scatter_fusion
  366.0 2.5 copy.158
  370.6 3.7 scatter_fusion
  378.3 2.3 select_add_fusion.2
  395.3 2.5 copy.158
  399.9 3.7 scatter_fusion
  407.5 2.3 select_add_fusion.2
  424.5 2.5 copy.158
  429.1 3.7 scatter_fusion
  436.7 2.3 select_add_fusion.2
  453.7 2.5 copy.158
  458.3 3.7 scatter_fusion
  465.9 2.3 select_add_fusion.2
  482.9 2.5 copy.158
  487.5 3.7 scatter_fusion
  495.2 2.3 select_add_fusion.2
  512.1 2.5 copy.158
  516.7 3.7 scatter_fusion
  524.4 2.3 select_add_fusion.2
  541.4 2.5 copy.158
  545.9 3.7 scatter_fusion
  553.6 2.3 select_add_fusion.2
  558.1 2.2 copy.119
  562.2 5.3 copy.120
  567.5 5.9 all-to-all-start.6
  573.4 9.5 %copy.115 = bf16[2048,2,128]{2,1,0:T(2,128)(2,1)} copy(bf16[2048,2,128]{2,0,1:T(8,128)(2,1)S(1)} %bitcast.244) | data formatting | bytes 2097152 | tf_op jit(solution)/shard_map/reshape | solution.py:185
  582.9 49.7 %all-to-all-done.6 = f32[16,2,128,256]{3,1,2,0:T(2,128)} async-done(((f32[16,2,128,256]{3,1,2,0:T(2,128)}), f32[16,2,128,256]{3,1,2,0:T(2,128)}, u32[]{:S(2)}, u32[]{:S(2)}) %all-to-all-start.6) | async-done | bytes 4194336 | tf_op jit(solution)/shard_map/all_to_all | solution.py:200
  632.5 12.4 %all-to-all-start.5 = ((bf16[2048,2,128]{2,1,0:T(2,128)(2,1)}), bf16[2048,2,128]{2,1,0:T(2,128)(2,1)}, u32[]{:S(2)}, u32[]{:S(2)}) async-start(bf16[2048,2,128]{2,1,0:T(2,128)(2,1)} %copy.115), calls=%async_computation.5 | async-start | bytes 2097152 | tf_op jit(solution)/shard_map/all_to_all | solution.py:186
  651.6 111.2 %all-reduce.7.cloned.1.call-done = f32[3,128,256]{2,0,1:T(4,128)} async-done(((f32[3,128,256]{2,0,1:T(4,128)}), f32[3,128,256]{2,0,1:T(4,128)}) %all-reduce.7.cloned.1.call-update) | async-done | bytes 393232 | tf_op jit(solution)/shard_map/psum | solution.py:203
  762.9 7.5 fusion.25
  771.6 10.0 %copy.125 = f32[2048,1,256]{2,1,0:T(1,128)} copy(f32[2048,1,256]{2,0,1:T(8,128)S(1)} %bitcast.231) | data formatting | bytes 4194304 | tf_op jit(solution)/shard_map/reshape | solution.py:212
  781.6 12.3 %all-to-all-start.7 = ((f32[2048,1,256]{2,1,0:T(1,128)}), f32[2048,1,256]{2,1,0:T(1,128)S(1)}, u32[]{:S(2)}, u32[]{:S(2)}) async-start(f32[2048,1,256]{2,1,0:T(1,128)} %copy.125), calls=%async_computation.7 | async-start | bytes 4194304 | tf_op jit(solution)/shard_map/all_to_all | solution.py:213
  797.1 87.2 %all-to-all-done.7 = f32[2048,1,256]{2,1,0:T(1,128)S(1)} async-done(((f32[2048,1,256]{2,1,0:T(1,128)}), f32[2048,1,256]{2,1,0:T(1,128)S(1)}, u32[]{:S(2)}, u32[]{:S(2)}) %all-to-all-start.7) | async-done | bytes 2097184 | tf_op jit(solution)/shard_map/all_to_all | solution.py:213
  (396 shorter events, 197.4 us)
Async XLA Ops:
  7.2 53.4 %copy-start = (s32[4,256,1]{1,2,0:T(1,128)S(1)}, s32[4,256,1]{1,2,0:T(1,128)}, u32[]{:S(2)}) copy-start(s32[4,256,1]{1,2,0:T(1,128)} %param.16) | copy-start | bytes 12292
  9.0 44.3 %all-to-all-start = ((bf16[128,16,128]{2,0,1:T(8,128)(2,1)}), bf16[128,16,128]{2,0,1:T(8,128)(2,1)S(1)}, u32[]{:S(2)}, u32[]{:S(2)}) async-start(bf16[128,16,128]{2,0,1:T(8,128)(2,1)} %bitcast.5), calls=%async_computation | async-start | bytes 1048576 | tf_op jit(solution)/shard_map/all_to_all | solution.py:68
  54.2 35.4 %all-to-all-start.1 = ((bf16[128,16,128]{2,0,1:T(8,128)(2,1)}), bf16[128,16,128]{2,0,1:T(8,128)(2,1)S(1)}, u32[]{:S(2)}, u32[]{:S(2)}) async-start(bf16[128,16,128]{2,0,1:T(8,128)(2,1)} %bitcast.9), calls=%async_computation.1 | async-start | bytes 1048576 | tf_op jit(solution)/shard_map/all_to_all | solution.py:69
  61.2 30.6 %copy-start.15 = (s32[16,2]{0,1:T(2,128)}, s32[16,2]{0,1:T(2,128)S(1)}, u32[]{:S(2)}) copy-start(s32[16,2]{0,1:T(2,128)S(1)} %select_reduce_fusion) | copy-start | bytes 388
  91.8 7.3 copy-start.9
  91.8 30.0 %all-to-all-start.2 = ((bf16[16,2,128,256]{3,2,1,0:T(8,128)(2,1)}), bf16[16,2,128,256]{3,2,1,0:T(8,128)(2,1)}, u32[]{:S(2)}, u32[]{:S(2)}) async-start(bf16[16,2,128,256]{3,2,1,0:T(8,128)(2,1)} %bitcast.19), calls=%async_computation.2 | async-start | bytes 4194304 | tf_op jit(solution)/shard_map/all_to_all | solution.py:103
  99.1 36.8 %copy-start.10 = (bf16[128,32,128]{2,1,0:T(8,128)(2,1)S(1)}, bf16[128,32,128]{2,1,0:T(8,128)(2,1)}, u32[]{:S(2)}) copy-start(bf16[128,32,128]{2,1,0:T(8,128)(2,1)} %param.15) | copy-start | bytes 3145732
  121.8 62.8 %all-to-all-start.3 = ((bf16[128,32,128]{2,0,1:T(8,128)(2,1)}), bf16[128,32,128]{2,0,1:T(8,128)(2,1)}, u32[]{:S(2)}, u32[]{:S(2)}) async-start(bf16[128,32,128]{2,0,1:T(8,128)(2,1)} %copy.112), calls=%async_computation.3 | async-start | bytes 2097152 | tf_op jit(solution)/shard_map/all_to_all | solution.py:67
  135.9 56.9 %copy-start.19 = (s32[4]{0:T(128)S(1)}, s32[4]{0:T(128)}, u32[]{:S(2)}) copy-start(s32[4]{0:T(128)} %param.17) | copy-start | bytes 52
  135.9 57.6 %copy-start.20 = (s32[4]{0:T(128)S(1)}, s32[4]{0:T(128)}, u32[]{:S(2)}) copy-start(s32[4]{0:T(128)} %param.18) | copy-start | bytes 52
  184.6 138.2 %all-to-all-start.4 = ((bf16[128,32,128]{2,0,1:T(8,128)(2,1)}), bf16[128,32,128]{2,0,1:T(8,128)(2,1)}, u32[]{:S(2)}, u32[]{:S(2)}) async-start(bf16[128,32,128]{2,0,1:T(8,128)(2,1)} %copy.113), calls=%async_computation.4 | async-start | bytes 2097152 | tf_op jit(solution)/shard_map/all_to_all | solution.py:70
  192.8 130.0 %all-reduce.5.cloned.1.call-start = ((), (), s32[]{:S(2)}) async-start(), calls=%async_computation.8 | async-start | bytes 393216 | tf_op jit(solution)/shard_map/psum | solution.py:16
  204.2 10.5 %collective-permute-start = (bf16[384,256]{1,0:T(8,128)(2,1)S(1)}, bf16[384,256]{1,0:T(8,128)(2,1)S(1)}, u32[]{:S(2)}, u32[]{:S(2)}) collective-permute-start(bf16[384,256]{1,0:T(8,128)(2,1)S(1)} %get-tuple-element.239), channel_id=1, source_target_pairs={{0,16},{16,32},{32,48},{48,64},{64,80},{80,96},{96,112},{112,128},... | collective-permute-start | bytes 589832 | tf_op jit(solution)/shard_map/ppermute | solution.py:22
  214.9 109.6 %copy-start.12 = (s32[8]{0:T(128)S(1)}, s32[8]{0:T(128)}, u32[]{:S(2)}) copy-start(s32[8]{0:T(128)} %constant.226) | copy-start | bytes 100
  324.5 3.1 copy-start.6
  349.2 4.4 copy-start.7
  349.2 4.4 copy-start.22
  353.6 3.1 copy-start.6
  378.3 4.5 copy-start.7
  378.3 4.5 copy-start.22
  382.8 3.1 copy-start.6
  407.5 4.5 copy-start.7
  407.5 4.5 copy-start.22
  412.1 3.1 copy-start.6
  436.7 4.5 copy-start.7
  436.7 4.5 copy-start.22
  441.3 3.1 copy-start.6
  465.9 4.5 copy-start.7
  465.9 4.5 copy-start.22
  470.5 3.1 copy-start.6
  495.2 4.5 copy-start.7
  495.2 4.5 copy-start.22
  499.7 3.1 copy-start.6
  524.4 4.5 copy-start.7
  524.4 4.5 copy-start.22
  528.9 3.1 copy-start.6
  553.6 4.5 copy-start.7
  553.6 4.5 copy-start.22
  567.5 5.9 copy-start.11
  567.5 65.0 %all-to-all-start.6 = ((f32[16,2,128,256]{3,1,2,0:T(2,128)}), f32[16,2,128,256]{3,1,2,0:T(2,128)}, u32[]{:S(2)}, u32[]{:S(2)}) async-start(f32[16,2,128,256]{3,1,2,0:T(2,128)} %copy.120), calls=%async_computation.6 | async-start | bytes 8388608 | tf_op jit(solution)/shard_map/all_to_all | solution.py:200
  573.4 71.5 %copy-start.4 = (f32[3,128,256]{1,0,2:T(4,128)S(1)}, f32[3,128,256]{1,0,2:T(4,128)}, u32[]{:S(2)}) copy-start(f32[3,128,256]{1,0,2:T(4,128)} %get-tuple-element.86) | copy-start | bytes 1179652
  582.9 63.1 %copy-start.3 = (f32[19,128,256]{2,1,0:T(8,128)S(1)}, f32[19,128,256]{2,1,0:T(8,128)}, u32[]{:S(2)}) copy-start(f32[19,128,256]{2,1,0:T(8,128)} %get-tuple-element.84) | copy-start | bytes 7471108
  632.5 149.1 %all-to-all-start.5 = ((bf16[2048,2,128]{2,1,0:T(2,128)(2,1)}), bf16[2048,2,128]{2,1,0:T(2,128)(2,1)}, u32[]{:S(2)}, u32[]{:S(2)}) async-start(bf16[2048,2,128]{2,1,0:T(2,128)(2,1)} %copy.115), calls=%async_computation.5 | async-start | bytes 2097152 | tf_op jit(solution)/shard_map/all_to_all | solution.py:186
  644.9 117.9 %all-reduce.7.cloned.1.call-start = ((), (), s32[]{:S(2)}) async-start(), calls=%async_computation.9 | async-start | bytes 1048576 | tf_op jit(solution)/shard_map/psum | solution.py:203
  646.0 5.4 copy-start.14
  649.2 113.7 %copy-start.16 = (s32[16,2]{0,1:T(2,128)S(1)}, s32[16,2]{0,1:T(2,128)}, u32[]{:S(2)}) copy-start(s32[16,2]{0,1:T(2,128)} %copy-done.15) | copy-start | bytes 388
  649.2 113.7 %collective-permute-start.1 = (f32[3,128,256]{2,0,1:T(4,128)S(1)}, f32[3,128,256]{2,0,1:T(4,128)S(1)}, u32[]{:S(2)}, u32[]{:S(2)}) collective-permute-start(f32[3,128,256]{2,0,1:T(4,128)S(1)} %slice.73), channel_id=1, source_target_pairs={{16,0},{32,16},{48,32},{64,48},{80,64},{96,80},{112,96},{128,112},... | collective-permute-start | bytes 1179656 | tf_op jit(solution)/shard_map/ppermute | solution.py:22
  781.6 102.7 %all-to-all-start.7 = ((f32[2048,1,256]{2,1,0:T(1,128)}), f32[2048,1,256]{2,1,0:T(1,128)S(1)}, u32[]{:S(2)}, u32[]{:S(2)}) async-start(f32[2048,1,256]{2,1,0:T(1,128)} %copy.125), calls=%async_computation.7 | async-start | bytes 4194304 | tf_op jit(solution)/shard_map/all_to_all | solution.py:213
  (22 other events, 44.3 us)
Sparse Core Ops, SparseCore 0:
  207.1 115.6 all-reduce.4
  649.0 113.7 all-reduce.6
where the time goes:
time: 900 us; the launch traced here: 893 us
  waiting for transfers between devices  486 us (54%)
  local copies, waits for them, and re-layouts  160 us (18%)
  starting transfers between devices  86 us (10%)
  other arithmetic  75.4 us (8%)
  matrix products  65 us (7%)
  between operations  14.6 us (2%)
    psum x1, waiting for transfers between devices, body(): sink_total = lax.psum(sink_sum, 'seq')  111 us
    psum x1, waiting for transfers between devices, spread(): return lax.psum(jnp.where(mine, array, jnp.zeros_like(array)), axis)  105 us
    all_to_all x1, waiting for transfers between devices, body(): lax.all_to_all(flat, 'head', split_axis=0, concat_axis=1, tiled=True)  87.2 us
    all_to_all x1, waiting for transfers between devices, body(): lax.all_to_all(outbound, 'seq', split_axis=0, concat_axis=0, tiled=True)  49.7 us
    all_to_all x1, waiting for transfers between devices, body(): lax.all_to_all(queries, 'head', split_axis=1, concat_axis=0, tiled=True)  47.3 us
    slice x16, local copies, waits for them, and re-layouts, turn(): window_terms = terms[:, SINK_MOST:SINK_MOST + WIN_MOST]  29.9 us
    scatter-add x8, other arithmetic, turn(): placed = jnp.zeros((span + reach, BLK, 2 * width), jnp.float32).at[window...  29.2 us
    all_to_all x1, waiting for transfers between devices, body(): lax.all_to_all(values_wide, 'head', split_axis=1, concat_axis=0, tiled=True)  28.2 us
  transfers between devices with their start and end apart: 12, of which 9 were waited for; matrix products, arithmetic and copies ran while one was open for 6% of the time, Pallas kernels for 0%

commit v1 on v0

v1 whole, which is shorter than its diff:
```python
import math

import jax
import jax.numpy as jnp
from jax import lax
from jax.experimental import pallas as pl
from jax.experimental.pallas import tpu as pltpu
from jax.sharding import PartitionSpec as P

BLK = 128
SINK_MOST = 3
WIN_MOST = 4
SLOTS = 8
N = 16
KVH = 4
GROUP = 8
HD = 128
CAP = 2
ROWS = 32
PIECE = (2, ROWS, HD)
MESH = pl.DeviceIdType.MESH
VMEM_LIMIT = 48 * 1024 * 1024


def remote(src, dst, send, recv, device):
    return pltpu.make_async_remote_copy(
        src_ref=src, dst_ref=dst, send_sem=send, recv_sem=recv, device_id=device, device_id_type=MESH
    )


def neighbours(seq, head):
    wrap_up = (head == N - 1).astype(jnp.int32)
    wrap_down = (head == 0).astype(jnp.int32)
    after = {"seq": lax.rem(seq + wrap_up, N), "head": lax.rem(head + 1, N)}
    before = {"seq": lax.rem(seq + N - wrap_down, N), "head": lax.rem(head + N - 1, N)}
    return before, after


def greet(seq, head, before, after):
    barrier = pltpu.get_barrier_semaphore()
    for k in range(1, N):
        pl.semaphore_signal(
            barrier, inc=1, device_id={"head": lax.rem(head + k, N)}, device_id_type=MESH
        )
        pl.semaphore_signal(
            barrier, inc=1, device_id={"seq": lax.rem(seq + k, N)}, device_id_type=MESH
        )
    pl.semaphore_signal(barrier, inc=1, device_id=before, device_id_type=MESH)
    pl.semaphore_signal(barrier, inc=1, device_id=after, device_id_type=MESH)
    pl.semaphore_wait(barrier, 2 * (N - 1) + 2)


def fetch_kernel(
    table, own, sink, win, kept,
    rows_in, slots_out, slots_in, far_out, piece, pieces,
    sw, rw, s1, r1, s2, r2, s3, r3, ss1, rs1, ss2, rs2, ss3, rs3,
):
    seq, head = lax.axis_index("seq"), lax.axis_index("head")
    before, after = neighbours(seq, head)
    greet(seq, head, before, after)

    steps = [remote(own, win.at[0], sw.at[0], rw.at[0], after)]
    for w in range(1, WIN_MOST - 1):
        steps.append(remote(win.at[w - 1], win.at[w], sw.at[w], rw.at[w], after))
    steps[0].start()

    def sink_send(k):
        return remote(own.at[k], piece, ss1.at[k], rs1.at[0], {"seq": k})

    @pl.when((seq == 0) & (head < SINK_MOST))
    def _():
        for k in range(1, N):
            sink_send(k).start()

    first = []
    for k in range(1, N):
        to = lax.rem(head + k, N)
        first.append(remote(own.at[to], rows_in.at[head], s1.at[k], r1.at[k], {"head": to}))
        first[-1].start()
    rows_in[head] = own[head]

    def piece_send(k):
        return remote(piece, pieces.at[head], ss2.at[k], rs2.at[head], {"head": lax.rem(head + k, N)})

    @pl.when((seq == 0) & (head < SINK_MOST))
    def _():
        piece[...] = own[0]

    @pl.when((seq > 0) & (head < SINK_MOST))
    def _():
        remote(own.at[0], piece, ss1.at[0], rs1.at[0], {"seq": 0}).wait_recv()

    @pl.when(head < SINK_MOST)
    def _():
        for k in range(1, N):
            piece_send(k).start()
        pieces[head] = piece[...]

    steps[0].wait_recv()
    steps[1].start()

    for copy in first:
        copy.wait_recv()
    for k in range(N):
        for c in range(CAP):
            slots_out[k, c] = rows_in[table[0, k * CAP + c]]
    second = []
    for k in range(1, N):
        to = lax.rem(seq + k, N)
        second.append(remote(slots_out.at[to], slots_in.at[seq], s2.at[k], r2.at[k], {"seq": to}))
        second[-1].start()
    slots_in[seq] = slots_out[seq]

    for b in range(SINK_MOST):

        @pl.when(head != b)
        def _():
            remote(piece, pieces.at[b], ss2.at[0], rs2.at[b], {"head": b}).wait_recv()

    spread = []
    for k in range(1, N):
        to = lax.rem(seq + k, N)
        spread.append(remote(pieces, sink.at[seq], ss3.at[k], rs3.at[k], {"seq": to}))
        spread[-1].start()
    sink[seq] = pieces[...]

    steps[1].wait_recv()
    steps[2].start()

    for copy in second:
        copy.wait_recv()
    for k in range(N):
        far_out[k] = slots_in[table[1, k], table[1, N + k]]
    third = []
    for k in range(1, N):
        to = lax.rem(head + k, N)
        third.append(remote(far_out.at[to], kept.at[head], s3.at[k], r3.at[k], {"head": to}))
        third[-1].start()
    kept[head] = far_out[head]

    steps[2].wait_recv()
    for copy in spread:
        copy.wait_recv()
    for copy in third:
        copy.wait_recv()
    for copy in steps + first + second + spread + third:
        copy.wait_send()

    @pl.when((seq == 0) & (head < SINK_MOST))
    def _():
        for k in range(1, N):
            sink_send(k).wait_send()

    @pl.when(head < SINK_MOST)
    def _():
        for k in range(1, N):
            piece_send(k).wait_send()


def fetch(table, own):
    sems = []
    for count in (3, N, N, N):
        sems += [pltpu.SemaphoreType.DMA((count,)), pltpu.SemaphoreType.DMA((count,))]
    sems += [pltpu.SemaphoreType.DMA((N,)), pltpu.SemaphoreType.DMA((1,))]
    sems += [pltpu.SemaphoreType.DMA((N,)), pltpu.SemaphoreType.DMA((N,))]
    sems += [pltpu.SemaphoreType.DMA((N,)), pltpu.SemaphoreType.DMA((N,))]
    vmem = pl.BlockSpec(memory_space=pltpu.VMEM)
    return pl.pallas_call(
        fetch_kernel,
        out_shape=(
            jax.ShapeDtypeStruct((N, SINK_MOST) + PIECE, jnp.bfloat16),
            jax.ShapeDtypeStruct((WIN_MOST - 1, N) + PIECE, jnp.bfloat16),
            jax.ShapeDtypeStruct((N,) + PIECE, jnp.bfloat16),
        ),
        in_specs=[pl.BlockSpec(memory_space=pltpu.SMEM), vmem],
        out_specs=(vmem, vmem, vmem),
        scratch_shapes=[
            pltpu.VMEM((N,) + PIECE, jnp.bfloat16),
            pltpu.VMEM((N, CAP) + PIECE, jnp.bfloat16),
            pltpu.VMEM((N, CAP) + PIECE, jnp.bfloat16),
            pltpu.VMEM((N,) + PIECE, jnp.bfloat16),
            pltpu.VMEM(PIECE, jnp.bfloat16),
            pltpu.VMEM((SINK_MOST,) + PIECE, jnp.bfloat16),
        ]
        + sems,
        compiler_params=pltpu.CompilerParams(
            collective_id=0, has_side_effects=True, vmem_limit_bytes=VMEM_LIMIT
        ),
        name="fetch",
    )(table, own)


def give_kernel(
    table, tsink, tkept, near, out,
    rows, slots_out, slots_in, run, back, back_in,
    sink_in, pieces, pieces_in, piece, whole, hop_out, hop_in, total,
    sw, rw, s1, r1, s2, r2, s3, r3, ss1, rs1, ss2, rs2, ss3, rs3,
):
    seq, head = lax.axis_index("seq"), lax.axis_index("head")
    before, after = neighbours(seq, head)
    greet(seq, head, before, after)
    low, wide = jnp.bfloat16, jnp.float32

    first = []
    for k in range(1, N):
        to = lax.rem(head + k, N)
        first.append(remote(tkept.at[to], rows.at[head], s1.at[k], r1.at[k], {"head": to}))
        first[-1].start()

    hop_out[0] = near[WIN_MOST - 1].astype(low)
    hops = [
        remote(hop_out.at[w], hop_in.at[w], sw.at[w], rw.at[w], before) for w in range(WIN_MOST - 1)
    ]
    hops[0].start()

    spread = []
    for k in range(1, N):
        to = lax.rem(seq + k, N)
        spread.append(remote(tsink.at[to], sink_in.at[seq], ss3.at[k], rs3.at[k], {"seq": to}))
        spread[-1].start()

    sink_in[seq] = tsink[seq]
    rows[head] = tkept[head]
    rows[N] = jnp.zeros(PIECE, low)

    for copy in first:
        copy.wait_recv()
    for k in range(N):
        for c in range(CAP):
            slots_out[k, c] = rows[table[2, k * CAP + c]]
    second = []
    for k in range(1, N):
        to = lax.rem(seq + k, N)
        second.append(remote(slots_out.at[to], slots_in.at[seq], s2.at[k], r2.at[k], {"seq": to}))
        second[-1].start()
    slots_in[seq] = slots_out[seq]

    hops[0].wait_recv()
    hop_out[1] = (near[2] + hop_in[0].astype(wide)).astype(low)
    hops[1].start()

    for copy in spread:
        copy.wait_recv()
    for b in range(SINK_MOST):
        term = sink_in[0, b].astype(wide)
        for k in range(1, N):
            term = term + sink_in[k, b].astype(wide)
        pieces[b] = term.astype(low)

    def piece_send(b):
        return remote(pieces.at[b], pieces_in.at[head], ss2.at[b], rs2.at[head], {"head": b})

    for b in range(SINK_MOST):

        @pl.when(head != b)
        def _():
            piece_send(b).start()

    run[...] = jnp.zeros(run.shape, wide)
    for copy in second:
        copy.wait_recv()
    for k in range(N):
        for c in range(CAP):
            i = k * CAP + c
            run[i] = slots_in[k, c].astype(wide) + run[table[3, i]]
    for k in range(N):
        back[k] = run[table[4, k]].astype(low)
    third = []
    for k in range(1, N):
        to = lax.rem(head + k, N)
        third.append(remote(back.at[to], back_in.at[head], s3.at[k], r3.at[k], {"head": to}))
        third[-1].start()
    back_in[head] = back[head]

    hops[1].wait_recv()
    hop_out[2] = (near[1] + hop_in[1].astype(wide)).astype(low)
    hops[2].start()

    def whole_send():
        return remote(piece, whole.at[seq], ss1.at[0], rs1.at[seq], {"seq": 0})

    @pl.when(head < SINK_MOST)
    def _():
        pieces_in[head] = pieces[head]
        for k in range(1, N):
            frm = lax.rem(head + k, N)
            remote(pieces.at[0], pieces_in.at[frm], ss2.at[0], rs2.at[frm], {"head": frm}).wait_recv()
        term = pieces_in[0].astype(wide)
        for k in range(1, N):
            term = term + pieces_in[k].astype(wide)
        piece[...] = term.astype(low)

    @pl.when((head < SINK_MOST) & (seq > 0))
    def _():
        whole_send().start()

    hops[2].wait_recv()
    total[...] = near[0] + hop_in[2].astype(wide)
    for copy in third:
        copy.wait_recv()
    total[...] = total[...] + back_in[...].astype(wide)

    @pl.when((head < SINK_MOST) & (seq == 0))
    def _():
        whole[0] = piece[...]
        for k in range(1, N):
            remote(piece, whole.at[k], ss1.at[0], rs1.at[k], {"seq": k}).wait_recv()
        total[...] = total[...] + whole[...].astype(wide)

    out[...] = total[...].astype(low)

    for copy in hops + first + second + spread + third:
        copy.wait_send()
    for b in range(SINK_MOST):

        @pl.when(head != b)
        def _():
            piece_send(b).wait_send()

    @pl.when((head < SINK_MOST) & (seq > 0))
    def _():
        whole_send().wait_send()


def give(table, tsink, tkept, near):
    sems = []
    for count in (3, N, N, N):
        sems += [pltpu.SemaphoreType.DMA((count,)), pltpu.SemaphoreType.DMA((count,))]
    sems += [pltpu.SemaphoreType.DMA((1,)), pltpu.SemaphoreType.DMA((N,))]
    sems += [pltpu.SemaphoreType.DMA((SINK_MOST,)), pltpu.SemaphoreType.DMA((N,))]
    sems += [pltpu.SemaphoreType.DMA((N,)), pltpu.SemaphoreType.DMA((N,))]
    vmem = pl.BlockSpec(memory_space=pltpu.VMEM)
    low, wide = jnp.bfloat16, jnp.float32
    return pl.pallas_call(
        give_kernel,
        out_shape=jax.ShapeDtypeStruct((N,) + PIECE, low),
        in_specs=[pl.BlockSpec(memory_space=pltpu.SMEM), vmem, vmem, vmem],
        out_specs=vmem,
        scratch_shapes=[
            pltpu.VMEM((N + 1,) + PIECE, low),
            pltpu.VMEM((N, CAP) + PIECE, low),
            pltpu.VMEM((N, CAP) + PIECE, low),
            pltpu.VMEM((N * CAP + 1,) + PIECE, wide),
            pltpu.VMEM((N,) + PIECE, low),
            pltpu.VMEM((N,) + PIECE, low),
            pltpu.VMEM((N, SINK_MOST) + PIECE, low),
            pltpu.VMEM((SINK_MOST,) + PIECE, low),
            pltpu.VMEM((N,) + PIECE, low),
            pltpu.VMEM(PIECE, low),
            pltpu.VMEM((N,) + PIECE, low),
            pltpu.VMEM((WIN_MOST - 1, N) + PIECE, low),
            pltpu.VMEM((WIN_MOST - 1, N) + PIECE, low),
            pltpu.VMEM((N,) + PIECE, wide),
        ]
        + sems,
        compiler_params=pltpu.CompilerParams(
            collective_id=1, has_side_effects=True, vmem_limit_bytes=VMEM_LIMIT
        ),
        name="give",
    )(table, tsink, tkept, near)


COLS = 256
PAIR = 2
NT = (((1,), (1,)), ((), ()))
NN = (((1,), (0,)), ((), ()))
TN = (((0,), (0,)), ((), ()))


def attend_kernel(
    bias, q, g, sink, own, win, kept, dq, tsink, tkept, near, kbuf, vbuf, qbuf, gbuf, pbuf, sbuf, dqbuf
):
    pair = pl.program_id(0)
    low, wide = jnp.bfloat16, jnp.float32
    scale = 1.0 / math.sqrt(HD)
    columns = BLK * GROUP

    for m in range(PAIR):
        rows = slice(m * GROUP, (m + 1) * GROUP)
        qbuf[...] = q[...].astype(wide)[:, rows].reshape(columns, HD).astype(low)
        gbuf[...] = g[...].astype(wide)[:, rows].reshape(columns, HD).astype(low)
        for j in range(4):
            r = m * 4 + j
            for side, buf in ((0, kbuf), (1, vbuf)):
                for slot in range(SLOTS):
                    if slot < SINK_MOST:
                        part = sink[r, slot, side]
                    elif slot == SINK_MOST:
                        part = own[r, side]
                    elif slot < SLOTS - 1:
                        part = win[slot - SINK_MOST - 1, r, side]
                    else:
                        part = kept[r, side]
                    buf[slot * BLK + j * ROWS : slot * BLK + (j + 1) * ROWS, :] = part

        def chunk(i, carry):
            at = pl.multiple_of(i * COLS, COLS)
            here = pl.ds(at, COLS)
            qc, gc = qbuf[here, :], gbuf[here, :]
            scores = []
            for slot in range(SLOTS):
                k = kbuf[slot * BLK : (slot + 1) * BLK, :]
                s = lax.dot_general(k, qc, NT, preferred_element_type=wide) * scale
                if slot == SINK_MOST:
                    u = lax.broadcasted_iota(jnp.int32, (BLK, COLS), 0)
                    t = (lax.broadcasted_iota(jnp.int32, (BLK, COLS), 1) + at) // GROUP
                    s = jnp.where(u <= t, s, -jnp.inf)
                else:
                    s = s + bias[(pair * PAIR + m) * SLOTS + slot]
                scores.append(s)
            top = scores[0]
            for s in scores[1:]:
                top = jnp.maximum(top, s)
            top = jnp.max(top, axis=0, keepdims=True)
            norm = jnp.zeros((BLK, COLS), wide)
            delta = jnp.zeros((BLK, COLS), wide)
            exps, grads = [], []
            for slot in range(SLOTS):
                v = vbuf[slot * BLK : (slot + 1) * BLK, :]
                e = jnp.exp(scores[slot] - top)
                d = lax.dot_general(v, gc, NT, preferred_element_type=wide)
                norm = norm + e
                delta = delta + e * d
                exps.append(e)
                grads.append(d)
            inverse = 1.0 / jnp.sum(norm, axis=0, keepdims=True)
            delta = jnp.sum(delta, axis=0, keepdims=True) * inverse
            for slot in range(SLOTS):
                p = exps[slot] * inverse
                pbuf[slot * BLK : (slot + 1) * BLK, here] = p.astype(low)
                sbuf[slot * BLK : (slot + 1) * BLK, here] = (p * (grads[slot] - delta)).astype(low)
            turned = lax.dot_general(kbuf[...], sbuf[:, here], TN, preferred_element_type=wide)
            tokens = pl.ds(pl.multiple_of(i * (COLS // GROUP), COLS // GROUP), COLS // GROUP)
            dqbuf[tokens, rows, :] = (turned.T * scale).reshape(COLS // GROUP, GROUP, HD)
            return carry

        lax.fori_loop(0, columns // COLS, chunk, 0)

        for slot in range(SLOTS):
            block = slice(slot * BLK, (slot + 1) * BLK)
            dk = lax.dot_general(sbuf[block, :], qbuf[...], NN, preferred_element_type=wide) * scale
            dv = lax.dot_general(pbuf[block, :], gbuf[...], NN, preferred_element_type=wide)
            for j in range(4):
                r = m * 4 + j
                for side, term in ((0, dk), (1, dv)):
                    part = term[j * ROWS : (j + 1) * ROWS]
                    if slot < SINK_MOST:
                        tsink[r, slot, side] = part.astype(low)
                    elif slot < SLOTS - 1:
                        near[slot - SINK_MOST, r, side] = part
                    else:
                        tkept[r, side] = part.astype(low)

    dq[...] = dqbuf[...].astype(low)


def attend(bias, q, g, sink, own, win, kept):
    low, wide = jnp.bfloat16, jnp.float32
    half = N // PAIR
    steps = KVH // PAIR
    tokens = pl.BlockSpec((BLK, PAIR * GROUP, HD), lambda i: (0, i, 0))
    sinks = pl.BlockSpec((half, SINK_MOST) + PIECE, lambda i: (i, 0, 0, 0, 0))
    block = pl.BlockSpec((half,) + PIECE, lambda i: (i, 0, 0, 0))

    def several(count):
        return pl.BlockSpec((count, half) + PIECE, lambda i: (0, i, 0, 0, 0))

    columns = BLK * GROUP
    return pl.pallas_call(
        attend_kernel,
        grid=(steps,),
        out_shape=(
            jax.ShapeDtypeStruct((BLK, KVH * GROUP, HD), low),
            jax.ShapeDtypeStruct((N, SINK_MOST) + PIECE, low),
            jax.ShapeDtypeStruct((N,) + PIECE, low),
            jax.ShapeDtypeStruct((WIN_MOST, N) + PIECE, wide),
        ),
        in_specs=[
            pl.BlockSpec(memory_space=pltpu.SMEM),
            tokens, tokens, sinks, block, several(WIN_MOST - 1), block,
        ],
        out_specs=(tokens, sinks, block, several(WIN_MOST)),
        scratch_shapes=[
            pltpu.VMEM((SLOTS * BLK, HD), low),
            pltpu.VMEM((SLOTS * BLK, HD), low),
            pltpu.VMEM((columns, HD), low),
            pltpu.VMEM((columns, HD), low),
            pltpu.VMEM((SLOTS * BLK, columns), low),
            pltpu.VMEM((SLOTS * BLK, columns), low),
            pltpu.VMEM((BLK, PAIR * GROUP, HD), wide),
        ],
        compiler_params=pltpu.CompilerParams(vmem_limit_bytes=VMEM_LIMIT),
        name="attend",
    )(bias, q, g, sink, own, win, kept)


def tables(kept_blocks, sink_blocks, window_blocks, seq, head):
    lists = lax.dynamic_index_in_dim(kept_blocks[:, :, 0], head // 4, 0, keepdims=False)
    lists = lists.reshape(N, N)
    owners, inner = lists // N, lists % N
    order = jnp.arange(N, dtype=jnp.int32)
    same = owners[:, :, None] == owners[:, None, :]
    ranks = jnp.sum((same & (order[None, :] < order[:, None])[None]).astype(jnp.int32), axis=2)
    places = jnp.arange(CAP, dtype=jnp.int32)
    match = (owners == seq)[:, None, :] & (ranks[:, None, :] == places[None, :, None])
    sent = jnp.sum(jnp.where(match, inner[:, None, :], 0), axis=2).reshape(N * CAP)
    valid = jnp.any(match, axis=2).reshape(N * CAP)
    my_owners = lax.dynamic_index_in_dim(owners, seq, 0, keepdims=False)
    my_ranks = lax.dynamic_index_in_dim(ranks, seq, 0, keepdims=False)
    mine = (my_owners[None, None, :] == order[:, None, None]) & (
        my_ranks[None, None, :] == places[None, :, None]
    )
    fill = N + jnp.sum(jnp.where(mine, order[None, None, :] - N, 0), axis=2).reshape(N * CAP)
    key = jnp.where(valid, sent, N)
    index = jnp.arange(N * CAP, dtype=jnp.int32)
    linked = (key[None, :] == key[:, None]) & (index[None, :] < index[:, None])
    none = N * CAP
    link = jnp.max(jnp.where(linked, index[None, :], -1), axis=1)
    link = jnp.where(link < 0, none, link)
    last = jnp.max(jnp.where(key[None, :] == order[:, None], index[None, :], -1), axis=1)
    last = jnp.where(last < 0, none, last)
    table = jnp.stack(
        [
            sent,
            jnp.concatenate([my_owners, my_ranks]),
            fill,
            link,
            jnp.concatenate([last, last]),
        ]
    )

    current = seq * N + head
    named = lax.dynamic_index_in_dim(kept_blocks[:, :, 0], current, 1, keepdims=True)
    sinks, windows = sink_blocks[:, None], window_blocks[:, None]
    ids = jnp.arange(SINK_MOST, dtype=jnp.int32)[None, :]
    sink_ok = (ids < sinks) & (ids <= current) & (current - ids >= windows)
    back = jnp.arange(WIN_MOST, dtype=jnp.int32)[None, :]
    window_ok = (back < windows) & (current - back >= 0)
    kept_ok = (named <= current) & (named >= sinks) & (current - named >= windows)
    allowed = jnp.concatenate([sink_ok, window_ok, kept_ok], axis=1)
    bias = jnp.where(allowed, 0.0, -jnp.inf).astype(jnp.float32).reshape(KVH * SLOTS)
    return table, bias


def body(queries, keys, values, out_grad, kept_blocks, sink_blocks, window_blocks):
    seq, head = lax.axis_index("seq"), lax.axis_index("head")
    table, bias = tables(kept_blocks, sink_blocks, window_blocks, seq, head)
    pair = jnp.stack([keys, values]).reshape(2, 4, ROWS, KVH, HD)
    own = jnp.transpose(pair, (3, 1, 0, 2, 4)).reshape((N,) + PIECE)
    sink, win, kept = fetch(table, own)
    dq, tsink, tkept, near = attend(bias, queries, out_grad, sink, own, win, kept)
    out = give(table, tsink, tkept, near)
    grads = jnp.transpose(out.reshape(KVH, 4, 2, ROWS, HD), (2, 1, 3, 0, 4))
    grads = grads.reshape(2, BLK, KVH, HD)
    return dq, grads[0], grads[1]


def solution(mesh):
    tokens = P(("dp", "seq", "head"), None, None)
    return jax.shard_map(
        body,
        mesh=mesh,
        in_specs=(tokens, tokens, tokens, tokens, P(), P(), P()),
        out_specs=(tokens, tokens, tokens),
        check_vma=False,
    )
```

time: 900 us -> 163 us (0.18)
  waiting for transfers between devices: 486 us -> 0 us
  local copies, waits for them, and re-layouts: 160 us -> 7.95 us
  Pallas kernels: 0 us -> 149 us
  starting transfers between devices: 86 us -> 0 us
  other arithmetic: 75.4 us -> 3.51 us
  matrix products: 65 us -> 0 us
  between operations: 14.6 us -> 0.83 us
    all_to_all x8 -> x0, waiting for transfers between devices: 262 us -> none  [the longest x1 87.2 us: body(): lax.all_to_all(flat, 'head', split_axis=0, concat_axis=1, tiled=True)]
    psum x2 -> x0, waiting for transfers between devices: 216 us -> none  [the longest x1 111 us: body(): sink_total = lax.psum(sink_sum, 'seq')]
    pallas_call x0 -> x3, Pallas kernels: none -> 149 us  [the longest x1 66.6 us: fetch(): pl.pallas_call(fetch_kernel, out_shape=(jax.ShapeDtypeStruct((N, SINK_MOS...]
    all_to_all x8 -> x0, starting transfers between devices: 81.6 us -> none  [the longest x1 15.2 us: body(): lax.all_to_all(keys_wide, 'head', split_axis=1, concat_axis=0, tiled=True)]
    dot_general x42 -> x0, matrix products: 65 us -> none  [the longest x8 11.3 us: turn(): jnp.einsum('bhtu,bthd->bud', probs_low, g_part, preferred_element_type=jn...]
    slice x26 -> x3, local copies, waits for them, and re-layouts: 31.9 us -> 1.54 us  [body(): return (dq, grads[0], grads[1])]
    scatter-add x8 -> x0, other arithmetic: 29.2 us -> none  [turn(): placed = jnp.zeros((span + reach, BLK, 2 * width), jnp.float32).at[window...]
    dynamic_update_slice x32 -> x0, local copies, waits for them, and re-layouts: 28.4 us -> none  [the longest x8 16 us: turn(): lax.dynamic_update_slice_in_dim(near_sum, previous + placed, position * s...]
  transfers between devices with their start and end apart: 12 -> 0, of which waited for: 9 -> 0; matrix products, arithmetic and copies ran while one was open for 6% -> 0% of each run, Pallas kernels for 0% -> 0%
where the time goes in v1:
time: 163 us; the launch traced here: 161 us
  Pallas kernels  149 us (91%)
  local copies, waits for them, and re-layouts  7.95 us (5%)
  other arithmetic  3.51 us (2%)
    pallas_call x1, Pallas kernels, fetch(): pl.pallas_call(fetch_kernel, out_shape=(jax.ShapeDtypeStruct((N, SINK_MOS...  66.6 us
    pallas_call x1, Pallas kernels, give(): pl.pallas_call(give_kernel, out_shape=jax.ShapeDtypeStruct((N,) + PIECE,...  54.5 us
    pallas_call x1, Pallas kernels, attend(): pl.pallas_call(attend_kernel, grid=(steps,), out_shape=(jax.ShapeDtypeStr...  27.7 us
    unnamed x8, local copies, waits for them, and re-layouts  3.47 us

profile of v1, /device:TPU:24, one launch (start us, length us, event | category | flops | bytes accessed | tf_op | source)
XLA Modules:
  0.0 161.1 jit_solution(11940352398626891785)
XLA Ops:
  0.6 0.0 copy-start
  0.6 0.0 copy-start.2
  0.7 0.6 copy-done
  1.3 0.2 dynamic-slice_reduce_fusion
  1.6 0.7 and_bitcast_fusion
  2.2 0.1 copy.20
  2.4 0.7 fusion.6
  3.1 0.7 fusion.7
  3.9 0.1 add_select_fusion.2
  4.0 0.1 select_n.100.bias
  4.0 0.1 reshape.261
  4.2 0.4 convert_reduce_fusion
  4.6 0.1 select_reduce_fusion.2
  4.7 0.1 fusion.1
  4.9 0.1 select_reduce_fusion.1
  5.0 0.1 copy.22
  5.1 0.1 add.68
  5.2 0.1 copy.21
  5.3 0.1 stack_reshape.3
  5.4 0.1 copy.23
  5.5 0.1 select_n.109
  5.6 0.1 select_reduce_fusion.3
  5.7 0.2 select_reduce_fusion
  5.9 0.1 add_bitcast_fusion
  6.0 0.9 copy.24
  6.9 0.9 copy.25
  7.9 66.6 %fetch.1 = (bf16[16,3,2,32,128]{4,3,2,1,0:T(8,128)(2,1)S(1)}, bf16[3,16,2,32,128]{4,3,2,1,0:T(8,128)(2,1)S(1)}, bf16[16,2,32,128]{3,2,1,0:T(8,128)(2,1)S(1)}) custom-call(s32[5,32]{1,0:T(8,128)S(1)} %stack.22.table, bf16[16,2,32,128]{3,2,1,0:T(8,128)(2,1)S(1)} %bitcast.22), custom_call_target="tpu_custom_call" | custom-call | tf_op jit(solution)/shard_map/fetch/pallas_call | solution.py:168
  74.5 0.0 copy-done.2
  74.5 0.0 copy-start.3
  74.5 1.2 copy-done.3
  75.8 27.7 %attend.1 = (bf16[128,32,128]{2,1,0:T(8,128)(2,1)}, bf16[16,3,2,32,128]{4,3,2,1,0:T(8,128)(2,1)S(1)}, bf16[16,2,32,128]{3,2,1,0:T(8,128)(2,1)S(1)}, f32[4,16,2,32,128]{4,3,2,1,0:T(8,128)}) custom-call(f32[32]{0:T(128)S(1)} %select_n.100.bias, bf16[128,32,128]{2,1,0:T(8,128)(2,1)S(1)} %copy-done.2, bf16[128,32,128]{2,1,0:T(8,128)(2,1)S(1)} %copy-done.3, ...), custom_call_target="tpu_custom_call" | custom-call | tf_op jit(solution)/shard_map/attend/pallas_call | solution.py:469
  103.4 0.0 copy-start.1
  103.5 1.6 copy-done.1
  105.0 54.5 %give.1 = bf16[16,2,32,128]{3,2,1,0:T(8,128)(2,1)S(1)} custom-call(s32[5,32]{1,0:T(8,128)S(1)} %stack.22.table, bf16[16,3,2,32,128]{4,3,2,1,0:T(8,128)(2,1)S(1)} %get-tuple-element.14.tsink, bf16[16,2,32,128]{3,2,1,0:T(8,128)(2,1)S(1)} %get-tuple-element.15.tkept, f32[4,16,2,32,128]{4,3,2,1,0:T(8,128)S(1)} %copy-done.1), custom_call_target="tpu_custom_call" | custom-call | tf_op jit(solution)/shard_map/give/pallas_call | solution.py:334
  159.6 0.8 copy.27
  160.3 0.8 copy.26
  (19 shorter events, 0.2 us)
Async XLA Ops:
  0.6 0.7 copy-start
  0.6 73.9 %copy-start.2 = (bf16[128,32,128]{2,1,0:T(8,128)(2,1)S(1)}, bf16[128,32,128]{2,1,0:T(8,128)(2,1)}, u32[]{:S(2)}) copy-start(bf16[128,32,128]{2,1,0:T(8,128)(2,1)} %q.1) | copy-start | bytes 3145732
  74.5 1.2 copy-start.3
  103.4 1.6 copy-start.1

commit v2 on v1

v2 whole, which is shorter than its diff:
```python
import math

import jax
import jax.numpy as jnp
from jax import lax
from jax.experimental import pallas as pl
from jax.experimental.pallas import tpu as pltpu
from jax.sharding import PartitionSpec as P

BLK = 128
SINK_MOST = 3
WIN_MOST = 4
SLOTS = 8
N = 16
KVH = 4
GROUP = 8
HD = 128
CAP = 2
ROWS = 32
PIECE = (2, ROWS, HD)
MESH = pl.DeviceIdType.MESH
VMEM_LIMIT = 60 * 1024 * 1024


def remote(src, dst, send, recv, device):
    return pltpu.make_async_remote_copy(
        src_ref=src, dst_ref=dst, send_sem=send, recv_sem=recv, device_id=device, device_id_type=MESH
    )


def neighbours(seq, head):
    wrap_up = (head == N - 1).astype(jnp.int32)
    wrap_down = (head == 0).astype(jnp.int32)
    after = {"seq": lax.rem(seq + wrap_up, N), "head": lax.rem(head + 1, N)}
    before = {"seq": lax.rem(seq + N - wrap_down, N), "head": lax.rem(head + N - 1, N)}
    return before, after


def greet(seq, head, before, after):
    barrier = pltpu.get_barrier_semaphore()
    for k in range(1, N):
        pl.semaphore_signal(
            barrier, inc=1, device_id={"head": lax.rem(head + k, N)}, device_id_type=MESH
        )
        pl.semaphore_signal(
            barrier, inc=1, device_id={"seq": lax.rem(seq + k, N)}, device_id_type=MESH
        )
    pl.semaphore_signal(barrier, inc=1, device_id=before, device_id_type=MESH)
    pl.semaphore_signal(barrier, inc=1, device_id=after, device_id_type=MESH)
    pl.semaphore_wait(barrier, 2 * (N - 1) + 2)


ORDER = [8] + [k for i in range(1, 8) for k in (i, N - i)]
COLS = 256
COLUMNS = BLK * GROUP
LOWEST = -1e30
NT = (((1,), (1,)), ((), ()))
NN = (((1,), (0,)), ((), ()))
TN = (((0,), (0,)), ((), ()))


def exchange(src, dst, send, recv, me, axis):
    copies = []
    for k in ORDER:
        to = lax.rem(me + k, N)
        copies.append(remote(src.at[to], dst.at[me], send.at[k], recv.at[k], {axis: to}))
        copies[-1].start()
    return copies


def kernel(
    table, bias, q_hbm, g_hbm, own, dq, out,
    rows_in, slots_out, slots_in, far_out, piece, pieces, sink, win, kept,
    tsink, tkept, near, rows, back_out, back_in, run, sums, sums_in,
    sink_in, shares, shares_in, share, whole, hop_out, hop_in, total,
    q_raw, g_raw, qbuf, gbuf, kbuf, ebuf, dbuf, sbuf, efar, dfar, tops, norms, deltas, factors, centre, dqbuf,
    load,
    sw, rw, s1, r1, s2, r2, s3, r3, ss1, rs1, ss2, rs2, ss3, rs3,
    tw, vw, t1, v1, t2, v2, t3, v3, ts1, vs1, ts2, vs2, ts3, vs3,
):
    seq, head = lax.axis_index("seq"), lax.axis_index("head")
    low, wide = jnp.bfloat16, jnp.float32
    scale = 1.0 / math.sqrt(HD)
    before, after = neighbours(seq, head)
    loads = [
        pltpu.make_async_copy(q_hbm, q_raw, load.at[0]),
        pltpu.make_async_copy(g_hbm, g_raw, load.at[1]),
    ]
    for copy in loads:
        copy.start()
    greet(seq, head, before, after)


    def part(ref, g, side):
        return ref[pl.ds(4 * g, 4), side].reshape(BLK, HD)

    def score(g, slot, k, v, e_ref, d_ref):
        kbuf[g, slot * BLK : (slot + 1) * BLK, :] = k
        for i in range(COLUMNS // COLS):
            here = slice(i * COLS, (i + 1) * COLS)
            s = lax.dot_general(k, qbuf[g, here, :], NT, preferred_element_type=wide) * scale
            if slot == SINK_MOST:
                u = lax.broadcasted_iota(jnp.int32, (BLK, COLS), 0)
                t = (lax.broadcasted_iota(jnp.int32, (BLK, COLS), 1) + i * COLS) // GROUP
                s = jnp.where(u <= t, s, -jnp.inf)
            else:
                s = s + bias[g * SLOTS + slot]
            top = jnp.maximum(jnp.max(s, axis=0, keepdims=True), LOWEST)
            e = jnp.exp(s - top)
            d = lax.dot_general(v, gbuf[g, here, :], NT, preferred_element_type=wide)
            e_ref[:, here] = e
            d_ref[:, here] = d
            tops[g, slot : slot + 1, here] = top
            norms[g, slot : slot + 1, here] = jnp.sum(e, axis=0, keepdims=True)
            deltas[g, slot : slot + 1, here] = jnp.sum(e * d, axis=0, keepdims=True)

    def score_all(slot, ref):
        def step(g, carry):
            score(g, slot, part(ref, g, 0), part(ref, g, 1), ebuf.at[g, slot], dbuf.at[g, slot])
            return carry

        lax.fori_loop(0, KVH, step, 0)

    def combine(g):
        t = tops[g]
        w = jnp.exp(t - jnp.max(t, axis=0, keepdims=True))
        inverse = 1.0 / jnp.sum(w * norms[g], axis=0, keepdims=True)
        factors[g] = w * inverse
        centre[g] = jnp.sum(w * deltas[g], axis=0, keepdims=True) * inverse

    def grad(g, slot, e_ref, d_ref, put):
        p = e_ref[...] * factors[g, slot : slot + 1, :]
        ds = (p * (d_ref[...] - centre[g])).astype(low)
        sbuf[g, slot * BLK : (slot + 1) * BLK, :] = ds
        put(0, (lax.dot_general(ds, qbuf[g], NN, preferred_element_type=wide) * scale).reshape(4, ROWS, HD))
        dv = lax.dot_general(p.astype(low), gbuf[g], NN, preferred_element_type=wide)
        put(1, dv.reshape(4, ROWS, HD))

    def grad_all(slot, put):
        def step(g, carry):
            grad(g, slot, ebuf.at[g, slot], dbuf.at[g, slot], lambda side, x: put(pl.ds(4 * g, 4), side, x))
            return carry

        lax.fori_loop(0, KVH, step, 0)


    first = exchange(own, rows_in, s1, r1, head, "head")

    def sink_send(k):
        return remote(own.at[k], piece, ss1.at[k], rs1.at[0], {"seq": k})

    @pl.when((seq == 0) & (head < SINK_MOST))
    def _():
        for k in range(1, N):
            sink_send(k).start()

    steps = [remote(own, win.at[0], sw.at[0], rw.at[0], after)]
    for w in range(1, WIN_MOST - 1):
        steps.append(remote(win.at[w - 1], win.at[w], sw.at[w], rw.at[w], after))
    steps[0].start()
    rows_in[head] = own[head]

    @pl.when((seq == 0) & (head < SINK_MOST))
    def _():
        piece[...] = own[0]

    for copy in loads:
        copy.wait()
    for raw, buf in ((q_raw, qbuf), (g_raw, gbuf)):
        for pair in range(KVH // 2):
            x = raw[:, 16 * pair : 16 * (pair + 1), :].astype(wide)
            for m in range(2):
                buf[2 * pair + m] = x[:, 8 * m : 8 * (m + 1)].reshape(COLUMNS, HD).astype(low)
    score_all(SINK_MOST, own)

    for copy in first:
        copy.wait_recv()
    for k in range(N):
        for c in range(CAP):
            slots_out[k, c] = rows_in[table[0, k * CAP + c]]
    second = exchange(slots_out, slots_in, s2, r2, seq, "seq")
    slots_in[seq] = slots_out[seq]

    def piece_send(k):
        return remote(piece, pieces.at[head], ss2.at[k], rs2.at[head], {"head": lax.rem(head + k, N)})

    @pl.when((seq > 0) & (head < SINK_MOST))
    def _():
        remote(own.at[0], piece, ss1.at[0], rs1.at[0], {"seq": 0}).wait_recv()

    @pl.when(head < SINK_MOST)
    def _():
        for k in ORDER:
            piece_send(k).start()
        pieces[head] = piece[...]

    steps[0].wait_recv()
    steps[1].start()
    score_all(SINK_MOST + 1, win.at[0])

    for copy in second:
        copy.wait_recv()
    for k in range(N):
        far_out[k] = slots_in[table[1, k], table[1, N + k]]
    third = exchange(far_out, kept, s3, r3, head, "head")
    kept[head] = far_out[head]

    steps[1].wait_recv()
    steps[2].start()
    score_all(SINK_MOST + 2, win.at[1])

    for b in range(SINK_MOST):

        @pl.when(head != b)
        def _():
            remote(piece, pieces.at[b], ss2.at[0], rs2.at[b], {"head": b}).wait_recv()

    spread = []
    for k in ORDER:
        to = lax.rem(seq + k, N)
        spread.append(remote(pieces, sink.at[seq], ss3.at[k], rs3.at[k], {"seq": to}))
        spread[-1].start()
    sink[seq] = pieces[...]

    steps[2].wait_recv()
    score_all(SINK_MOST + 3, win.at[2])
    for copy in spread:
        copy.wait_recv()
    for b in range(SINK_MOST):

        def step(g, carry):
            k = sink[pl.ds(4 * g, 4), b, 0].reshape(BLK, HD)
            v = sink[pl.ds(4 * g, 4), b, 1].reshape(BLK, HD)
            score(g, b, k, v, ebuf.at[g, b], dbuf.at[g, b])
            return carry

        lax.fori_loop(0, KVH, step, 0)
    for copy in third:
        copy.wait_recv()


    def kept_step(g, carry):
        score(g, SLOTS - 1, part(kept, g, 0), part(kept, g, 1), efar, dfar)
        combine(g)

        def put(side, x):
            tkept[pl.ds(4 * g, 4), side] = x.astype(low)

        grad(g, SLOTS - 1, efar, dfar, put)
        return carry

    lax.fori_loop(0, KVH, kept_step, 0)
    first_back = exchange(tkept, rows, t1, v1, head, "head")
    rows[head] = tkept[head]
    rows[N] = jnp.zeros(PIECE, low)

    def put_hop(at, side, x):
        hop_out[0, at, side] = x.astype(low)

    grad_all(SLOTS - 2, put_hop)
    hops = [
        remote(hop_out.at[w], hop_in.at[w], tw.at[w], vw.at[w], before) for w in range(WIN_MOST - 1)
    ]
    hops[0].start()

    for b in range(SINK_MOST):

        def put_sink(at, side, x):
            tsink[at, b, side] = x.astype(low)

        grad_all(b, put_sink)
    spread_back = exchange(tsink, sink_in, ts3, vs3, seq, "seq")
    sink_in[seq] = tsink[seq]

    def put_near(n):
        def put(at, side, x):
            near[n, at, side] = x

        return put

    grad_all(SINK_MOST + 2, put_near(2))

    for copy in first_back:
        copy.wait_recv()
    for k in range(N):
        for c in range(CAP):
            back_out[k, c] = rows[table[2, k * CAP + c]]
    second_back = exchange(back_out, back_in, t2, v2, seq, "seq")
    back_in[seq] = back_out[seq]

    hops[0].wait_recv()
    hop_out[1] = (near[2] + hop_in[0].astype(wide)).astype(low)
    hops[1].start()
    grad_all(SINK_MOST + 1, put_near(1))

    for copy in spread_back:
        copy.wait_recv()
    for b in range(SINK_MOST):
        term = sink_in[0, b].astype(wide)
        for k in range(1, N):
            term = term + sink_in[k, b].astype(wide)
        shares[b] = term.astype(low)

    def share_send(b):
        return remote(shares.at[b], shares_in.at[head], ts2.at[b], vs2.at[head], {"head": b})

    for b in range(SINK_MOST):

        @pl.when(head != b)
        def _():
            share_send(b).start()

    run[...] = jnp.zeros(run.shape, wide)
    for copy in second_back:
        copy.wait_recv()
    for k in range(N):
        for c in range(CAP):
            i = k * CAP + c
            run[i] = back_in[k, c].astype(wide) + run[table[3, i]]
    for k in range(N):
        sums[k] = run[table[4, k]].astype(low)
    third_back = exchange(sums, sums_in, t3, v3, head, "head")
    sums_in[head] = sums[head]

    hops[1].wait_recv()
    hop_out[2] = (near[1] + hop_in[1].astype(wide)).astype(low)
    hops[2].start()
    grad_all(SINK_MOST, put_near(0))

    def whole_send():
        return remote(share, whole.at[seq], ts1.at[0], vs1.at[seq], {"seq": 0})

    @pl.when(head < SINK_MOST)
    def _():
        shares_in[head] = shares[head]
        for k in range(1, N):
            frm = lax.rem(head + k, N)
            remote(shares.at[0], shares_in.at[frm], ts2.at[0], vs2.at[frm], {"head": frm}).wait_recv()
        term = shares_in[0].astype(wide)
        for k in range(1, N):
            term = term + shares_in[k].astype(wide)
        share[...] = term.astype(low)

    @pl.when((head < SINK_MOST) & (seq > 0))
    def _():
        whole_send().start()

    for g in range(KVH):
        turned = lax.dot_general(kbuf[g], sbuf[g], TN, preferred_element_type=wide)
        m = g % 2
        dqbuf[:, GROUP * m : GROUP * (m + 1), :] = (turned.T * scale).reshape(BLK, GROUP, HD)
        if m == 1:
            dq[:, GROUP * (g - 1) : GROUP * (g + 1), :] = dqbuf[...].astype(low)

    hops[2].wait_recv()
    total[...] = near[0] + hop_in[2].astype(wide)
    for copy in third_back:
        copy.wait_recv()
    total[...] = total[...] + sums_in[...].astype(wide)

    @pl.when((head < SINK_MOST) & (seq == 0))
    def _():
        whole[0] = share[...]
        for k in range(1, N):
            remote(share, whole.at[k], ts1.at[0], vs1.at[k], {"seq": k}).wait_recv()
        total[...] = total[...] + whole[...].astype(wide)

    out[...] = total[...].astype(low)


    for copy in steps + first + second + third + spread:
        copy.wait_send()
    for copy in hops + first_back + second_back + third_back + spread_back:
        copy.wait_send()

    @pl.when((seq == 0) & (head < SINK_MOST))
    def _():
        for k in range(1, N):
            sink_send(k).wait_send()

    @pl.when(head < SINK_MOST)
    def _():
        for k in ORDER:
            piece_send(k).wait_send()

    for b in range(SINK_MOST):

        @pl.when(head != b)
        def _():
            share_send(b).wait_send()

    @pl.when((head < SINK_MOST) & (seq > 0))
    def _():
        whole_send().wait_send()


def attend(table, bias, q, g, own):
    low, wide = jnp.bfloat16, jnp.float32
    vmem = pl.BlockSpec(memory_space=pltpu.VMEM)
    smem = pl.BlockSpec(memory_space=pltpu.SMEM)
    hbm = pl.BlockSpec(memory_space=pl.ANY)
    dma = pltpu.SemaphoreType.DMA

    def lows(*lead):
        return pltpu.VMEM(lead + PIECE, low)

    def wides(*lead):
        return pltpu.VMEM(lead + PIECE, wide)

    raw = pltpu.VMEM((BLK, KVH * GROUP, HD), low)
    flat = pltpu.VMEM((KVH, COLUMNS, HD), low)
    rows = pltpu.VMEM((KVH, SLOTS, COLUMNS), wide)
    return pl.pallas_call(
        kernel,
        out_shape=(
            jax.ShapeDtypeStruct((BLK, KVH * GROUP, HD), low),
            jax.ShapeDtypeStruct((N,) + PIECE, low),
        ),
        in_specs=[smem, smem, hbm, hbm, vmem],
        out_specs=(vmem, vmem),
        scratch_shapes=[
            lows(N), lows(N, CAP), lows(N, CAP), lows(N), lows(), lows(SINK_MOST),
            lows(N, SINK_MOST), lows(WIN_MOST - 1, N), lows(N),
            lows(N, SINK_MOST), lows(N), wides(WIN_MOST - 1, N), lows(N + 1), lows(N, CAP), lows(N, CAP),
            wides(N * CAP + 1), lows(N), lows(N),
            lows(N, SINK_MOST), lows(SINK_MOST), lows(N), lows(), lows(N),
            lows(WIN_MOST - 1, N), lows(WIN_MOST - 1, N), wides(N),
            raw, raw, flat, flat,
            pltpu.VMEM((KVH, SLOTS * BLK, HD), low),
            pltpu.VMEM((KVH, SLOTS - 1, BLK, COLUMNS), wide),
            pltpu.VMEM((KVH, SLOTS - 1, BLK, COLUMNS), wide),
            pltpu.VMEM((KVH, SLOTS * BLK, COLUMNS), low),
            pltpu.VMEM((BLK, COLUMNS), wide),
            pltpu.VMEM((BLK, COLUMNS), wide),
            rows, rows, rows, rows,
            pltpu.VMEM((KVH, 1, COLUMNS), wide),
            pltpu.VMEM((BLK, 2 * GROUP, HD), wide),
            dma((2,)),
            dma((3,)), dma((3,)), dma((N,)), dma((N,)), dma((N,)), dma((N,)), dma((N,)), dma((N,)),
            dma((N,)), dma((1,)), dma((N,)), dma((N,)), dma((N,)), dma((N,)),
            dma((3,)), dma((3,)), dma((N,)), dma((N,)), dma((N,)), dma((N,)), dma((N,)), dma((N,)),
            dma((1,)), dma((N,)), dma((SINK_MOST,)), dma((N,)), dma((N,)), dma((N,)),
        ],
        compiler_params=pltpu.CompilerParams(
            collective_id=0, has_side_effects=True, vmem_limit_bytes=VMEM_LIMIT
        ),
        name="attend",
    )(table, bias, q, g, own)


def tables(kept_blocks, sink_blocks, window_blocks, seq, head):
    lists = lax.dynamic_index_in_dim(kept_blocks[:, :, 0], head // 4, 0, keepdims=False)
    lists = lists.reshape(N, N)
    owners, inner = lists // N, lists % N
    order = jnp.arange(N, dtype=jnp.int32)
    same = owners[:, :, None] == owners[:, None, :]
    ranks = jnp.sum((same & (order[None, :] < order[:, None])[None]).astype(jnp.int32), axis=2)
    places = jnp.arange(CAP, dtype=jnp.int32)
    match = (owners == seq)[:, None, :] & (ranks[:, None, :] == places[None, :, None])
    sent = jnp.sum(jnp.where(match, inner[:, None, :], 0), axis=2).reshape(N * CAP)
    valid = jnp.any(match, axis=2).reshape(N * CAP)
    my_owners = lax.dynamic_index_in_dim(owners, seq, 0, keepdims=False)
    my_ranks = lax.dynamic_index_in_dim(ranks, seq, 0, keepdims=False)
    mine = (my_owners[None, None, :] == order[:, None, None]) & (
        my_ranks[None, None, :] == places[None, :, None]
    )
    fill = N + jnp.sum(jnp.where(mine, order[None, None, :] - N, 0), axis=2).reshape(N * CAP)
    key = jnp.where(valid, sent, N)
    index = jnp.arange(N * CAP, dtype=jnp.int32)
    linked = (key[None, :] == key[:, None]) & (index[None, :] < index[:, None])
    none = N * CAP
    link = jnp.max(jnp.where(linked, index[None, :], -1), axis=1)
    link = jnp.where(link < 0, none, link)
    last = jnp.max(jnp.where(key[None, :] == order[:, None], index[None, :], -1), axis=1)
    last = jnp.where(last < 0, none, last)
    table = jnp.stack(
        [
            sent,
            jnp.concatenate([my_owners, my_ranks]),
            fill,
            link,
            jnp.concatenate([last, last]),
        ]
    )

    current = seq * N + head
    named = lax.dynamic_index_in_dim(kept_blocks[:, :, 0], current, 1, keepdims=True)
    sinks, windows = sink_blocks[:, None], window_blocks[:, None]
    ids = jnp.arange(SINK_MOST, dtype=jnp.int32)[None, :]
    sink_ok = (ids < sinks) & (ids <= current) & (current - ids >= windows)
    back = jnp.arange(WIN_MOST, dtype=jnp.int32)[None, :]
    window_ok = (back < windows) & (current - back >= 0)
    kept_ok = (named <= current) & (named >= sinks) & (current - named >= windows)
    allowed = jnp.concatenate([sink_ok, window_ok, kept_ok], axis=1)
    bias = jnp.where(allowed, 0.0, -jnp.inf).astype(jnp.float32).reshape(KVH * SLOTS)
    return table, bias


def body(queries, keys, values, out_grad, kept_blocks, sink_blocks, window_blocks):
    seq, head = lax.axis_index("seq"), lax.axis_index("head")
    table, bias = tables(kept_blocks, sink_blocks, window_blocks, seq, head)
    pair = jnp.stack([keys, values]).reshape(2, 4, ROWS, KVH, HD)
    own = jnp.transpose(pair, (3, 1, 0, 2, 4)).reshape((N,) + PIECE)
    dq, out = attend(table, bias, queries, out_grad, own)
    grads = jnp.transpose(out.reshape(KVH, 4, 2, ROWS, HD), (2, 1, 3, 0, 4))
    grads = grads.reshape(2, BLK, KVH, HD)
    return dq, grads[0], grads[1]


def solution(mesh):
    tokens = P(("dp", "seq", "head"), None, None)
    return jax.shard_map(
        body,
        mesh=mesh,
        in_specs=(tokens, tokens, tokens, tokens, P(), P(), P()),
        out_specs=(tokens, tokens, tokens),
        check_vma=False,
    )
```

time: 163 us -> 134 us (0.82)
  the two profiles are of different devices: /device:TPU:24 before, /device:TPU:66 now
where the time goes in v2:
time: 134 us
  Pallas kernels  123 us (92%)
  local copies, waits for them, and re-layouts  7.33 us (5%)
  other arithmetic  2.2 us (2%)
    pallas_call x1, Pallas kernels, attend(): pl.pallas_call(kernel, out_shape=(jax.ShapeDtypeStruct((BLK, KVH * GROUP,...  123 us

profile of v2, /device:TPU:66, one launch (start us, length us, event | category | flops | bytes accessed | tf_op | source)
XLA Modules:
  0.0 133.6 jit_solution(13476396817834407746)
XLA Ops:
  0.6 0.0 copy-start
  0.7 0.0 copy-start.4
  0.7 0.0 copy-start.5
  0.7 0.0 copy-start.2
  0.7 0.6 copy-done
  1.3 0.2 dynamic-slice_reduce_fusion
  1.6 0.0 copy-done.4
  1.6 0.0 copy-done.5
  1.6 0.1 copy.23
  1.7 0.1 fusion.6
  1.8 0.1 fusion.7
  1.9 0.1 add_select_fusion.2
  2.0 0.6 select_n.113.bias
  2.6 0.1 reshape.261
  2.7 0.4 convert_reduce_fusion
  3.1 0.1 select_reduce_fusion.2
  3.3 0.1 fusion.1
  3.4 0.1 select_reduce_fusion.1
  3.6 0.1 copy.21
  3.6 0.1 add.66
  3.7 0.1 copy.20
  3.8 0.1 stack_reshape.3
  3.9 0.1 copy.22
  4.0 0.1 select_n.106
  4.1 0.1 select_reduce_fusion.3
  4.2 0.2 select_reduce_fusion
  4.4 0.1 add_bitcast_fusion
  4.5 0.6 stack.22.table
  5.1 0.0 copy-done.2
  5.1 0.0 copy-start.3
  5.1 0.9 copy-done.3
  6.0 0.7 pad_maximum_fusion
  6.8 123.2 %attend.1 = (bf16[128,32,128]{2,1,0:T(8,128)(2,1)}, bf16[16,2,32,128]{3,2,1,0:T(8,128)(2,1)}) custom-call(s32[5,32]{1,0:T(8,128)} %stack.22.table, f32[32]{0:T(128)} %select_n.113.bias, bf16[128,32,128]{2,1,0:T(8,128)(2,1)} %q_hbm.1, bf16[128,32,128]{2,1,0:T(8,128)(2,1)} %g_hbm.1, bf16[16,2,32,128]{3,2,1,0:T(8,128)(2,1)} %bitcast.22), custom_call_target="tpu_custom_call" | custom-call | tf_op jit(solution)/shard_map/attend/pallas_call | solution.py:413
  130.0 0.0 copy-start.1
  130.0 1.1 fusion.10
  131.1 0.8 copy.27
  131.9 0.8 copy.26
  132.6 0.0 copy-done.1
  132.6 1.0 copy.29
  (19 shorter events, 0.2 us)
Async XLA Ops:
  0.6 0.7 copy-start
  0.7 0.9 copy-start.4
  0.7 0.9 copy-start.5
  0.7 4.4 %copy-start.2 = (bf16[128,4,128]{2,1,0:T(4,128)(2,1)S(1)}, bf16[128,4,128]{2,1,0:T(4,128)(2,1)}, u32[]{:S(2)}) copy-start(bf16[128,4,128]{2,1,0:T(4,128)(2,1)} %param.8) | copy-start | bytes 393220
  5.1 0.9 copy-start.3
  130.0 2.6 %copy-start.1 = (bf16[128,32,128]{2,1,0:T(8,128)(2,1)S(1)}, bf16[128,32,128]{2,1,0:T(8,128)(2,1)}, u32[]{:S(2)}) copy-start(bf16[128,32,128]{2,1,0:T(8,128)(2,1)} %get-tuple-element.16) | copy-start | bytes 3145732

commit v3 on v2

v3 whole, which is shorter than its diff:
```python
import math

import jax
import jax.numpy as jnp
from jax import lax
from jax.experimental import pallas as pl
from jax.experimental.pallas import tpu as pltpu
from jax.sharding import PartitionSpec as P

BLK = 128
SINK_MOST = 3
WIN_MOST = 4
SLOTS = 8
N = 16
KVH = 4
GROUP = 8
HD = 128
CAP = 2
ROWS = 32
PIECE = (2, ROWS, HD)
MESH = pl.DeviceIdType.MESH
VMEM_LIMIT = 60 * 1024 * 1024


def remote(src, dst, send, recv, device):
    return pltpu.make_async_remote_copy(
        src_ref=src, dst_ref=dst, send_sem=send, recv_sem=recv, device_id=device, device_id_type=MESH
    )


def neighbours(seq, head):
    wrap_up = (head == N - 1).astype(jnp.int32)
    wrap_down = (head == 0).astype(jnp.int32)
    after = {"seq": lax.rem(seq + wrap_up, N), "head": lax.rem(head + 1, N)}
    before = {"seq": lax.rem(seq + N - wrap_down, N), "head": lax.rem(head + N - 1, N)}
    return before, after


def greet(seq, head, before, after):
    barrier = pltpu.get_barrier_semaphore()
    for k in range(1, N):
        pl.semaphore_signal(
            barrier, inc=1, device_id={"head": lax.rem(head + k, N)}, device_id_type=MESH
        )
        pl.semaphore_signal(
            barrier, inc=1, device_id={"seq": lax.rem(seq + k, N)}, device_id_type=MESH
        )
    pl.semaphore_signal(barrier, inc=1, device_id=before, device_id_type=MESH)
    pl.semaphore_signal(barrier, inc=1, device_id=after, device_id_type=MESH)
    pl.semaphore_wait(barrier, 2 * (N - 1) + 2)


ORDER = [8] + [k for i in range(1, 8) for k in (i, N - i)]
COLS = 256
CHUNKS = 2
NEAR = (2, 1, N - 1)
COLUMNS = BLK * GROUP
LOWEST = -1e30
NT = (((1,), (1,)), ((), ()))
NN = (((1,), (0,)), ((), ()))
TN = (((0,), (0,)), ((), ()))


def exchange(src, dst, send, recv, me, axis):
    copies = []
    for k in ORDER:
        to = lax.rem(me + k, N)
        copies.append(remote(src.at[to], dst.at[me], send.at[k], recv.at[k], {axis: to}))
        copies[-1].start()
    return copies


def kernel(
    kept_blocks, sink_blocks, window_blocks, q_hbm, g_hbm, keys, values, dq, dk, dv,
    own, rows_in, slots_out, slots_in, far_out, piece, pieces, sink, win, kept,
    tsink, tkept, near, rows, back_out, back_in, run, sums, sums_in,
    sink_in, shares, shares_in, shares_far, share, whole_out, whole, hop_out, hop_in, total,
    q_raw, g_raw, qbuf, gbuf, kbuf, ebuf, dbuf, sbuf, efar, dfar, tops, norms, deltas, factors, centre, dqbuf,
    marks, fills, links, lasts, load,
    sw, rw, s1, r1, s2, r2, s3, r3, ss1, rs1, ss2, rs2, ss3, rs3,
    tw, vw, t1, v1, t2, v2, t3, v3, ts1, vs1, ts2, vs2, ts3, vs3,
):
    seq, head = lax.axis_index("seq"), lax.axis_index("head")
    low, wide = jnp.bfloat16, jnp.float32
    scale = 1.0 / math.sqrt(HD)
    before, after = neighbours(seq, head)
    loads = [
        pltpu.make_async_copy(q_hbm, q_raw, load.at[0]),
        pltpu.make_async_copy(g_hbm, g_raw, load.at[1]),
    ]
    for copy in loads:
        copy.start()
    for side, ref in ((0, keys), (1, values)):
        x = ref[...].astype(wide)
        for g in range(KVH):
            own[4 * g : 4 * (g + 1), side] = x[:, g, :].astype(low).reshape(4, ROWS, HD)
    greet(seq, head, before, after)


    current = seq * N + head

    def allowed(g, slot):
        sinks, windows = sink_blocks[g], window_blocks[g]
        if slot < SINK_MOST:
            return (slot < sinks) & (slot <= current) & (current - slot >= windows)
        if slot < SLOTS - 1:
            return (slot - SINK_MOST < windows) & (slot - SINK_MOST <= current)
        named = kept_blocks[g, current]
        return (named <= current) & (named >= sinks) & (current - named >= windows)

    def part(ref, g, side):
        return ref[pl.ds(4 * g, 4), side].reshape(BLK, HD)

    def score(g, slot, k, v, e_ref, d_ref):
        kbuf[g, slot * BLK : (slot + 1) * BLK, :] = k
        bias = jnp.where(allowed(g, slot), 0.0, -jnp.inf)
        for i in range(COLUMNS // COLS):
            here = slice(i * COLS, (i + 1) * COLS)
            s = lax.dot_general(k, qbuf[g, here, :], NT, preferred_element_type=wide) * scale
            if slot == SINK_MOST:
                u = lax.broadcasted_iota(jnp.int32, (BLK, COLS), 0)
                t = (lax.broadcasted_iota(jnp.int32, (BLK, COLS), 1) + i * COLS) // GROUP
                s = jnp.where(u <= t, s, -jnp.inf)
            else:
                s = s + bias
            top = jnp.maximum(jnp.max(s, axis=0, keepdims=True), LOWEST)
            e = jnp.exp(s - top)
            d = lax.dot_general(v, gbuf[g, here, :], NT, preferred_element_type=wide)
            e_ref[:, here] = e
            d_ref[:, here] = d
            tops[g, slot : slot + 1, here] = top
            norms[g, slot : slot + 1, here] = jnp.sum(e, axis=0, keepdims=True)
            deltas[g, slot : slot + 1, here] = jnp.sum(e * d, axis=0, keepdims=True)

    def score_all(slot, ref):
        def step(g, carry):
            score(g, slot, part(ref, g, 0), part(ref, g, 1), ebuf.at[g, slot], dbuf.at[g, slot])
            return carry

        lax.fori_loop(0, KVH, step, 0)

    def combine(g):
        t = tops[g]
        w = jnp.exp(t - jnp.max(t, axis=0, keepdims=True))
        inverse = 1.0 / jnp.sum(w * norms[g], axis=0, keepdims=True)
        factors[g] = w * inverse
        centre[g] = jnp.sum(w * deltas[g], axis=0, keepdims=True) * inverse

    def grad(g, slot, e_ref, d_ref, put):
        p = e_ref[...] * factors[g, slot : slot + 1, :]
        ds = (p * (d_ref[...] - centre[g])).astype(low)
        sbuf[g, slot * BLK : (slot + 1) * BLK, :] = ds
        put(0, (lax.dot_general(ds, qbuf[g], NN, preferred_element_type=wide) * scale).reshape(4, ROWS, HD))
        dv = lax.dot_general(p.astype(low), gbuf[g], NN, preferred_element_type=wide)
        put(1, dv.reshape(4, ROWS, HD))

    def grad_all(slot, put):
        def step(g, carry):
            grad(g, slot, ebuf.at[g, slot], dbuf.at[g, slot], lambda side, x: put(pl.ds(4 * g, 4), side, x))
            return carry

        lax.fori_loop(0, KVH, step, 0)


    group = head // 4
    nowhere = N * CAP

    def mark(d, carry):
        first, second = jnp.int32(N), jnp.int32(N)
        for p in range(N):
            entry = kept_blocks[group, d * N + p]
            inner = jnp.where((entry >> 4) == seq, entry & (N - 1), N)
            second = jnp.where(first < N, jnp.where(second < N, second, inner), second)
            first = jnp.where(first < N, first, inner)
        marks[CAP * d] = first
        marks[CAP * d + 1] = second
        return carry

    def places():
        owners = [kept_blocks[group, seq * N + p] >> 4 for p in range(N)]
        found = []
        for p in range(N):
            rank = jnp.int32(0)
            for r in range(p):
                rank = rank + jnp.where(owners[r] == owners[p], 1, 0)
            found.append(CAP * owners[p] + rank)
        return found

    def fill(i, carry):
        which = jnp.int32(N)
        for p in range(N):
            which = jnp.where(slot_of[p] == i, p, which)
        fills[i] = which
        return carry

    def link(i, carry):
        which, key = jnp.int32(nowhere), marks[i]
        for r in range(N * CAP):
            which = jnp.where((marks[r] == key) & (r < i), r, which)
        links[i] = which
        return carry

    def last(z, carry):
        which = jnp.int32(nowhere)
        for r in range(N * CAP):
            which = jnp.where(marks[r] == z, r, which)
        lasts[z] = which
        return carry


    first = exchange(own, rows_in, s1, r1, head, "head")

    def sink_send(k):
        return remote(own.at[k], piece, ss1.at[k], rs1.at[0], {"seq": k})

    @pl.when((seq == 0) & (head < SINK_MOST))
    def _():
        for k in range(1, N):
            sink_send(k).start()

    steps = []

    def relay(w):
        for c in range(CHUNKS):
            at = pl.ds(c * (N // CHUNKS), N // CHUNKS)
            i = w * CHUNKS + c
            src = own.at[at] if w == 0 else win.at[w - 1, at]
            if w > 0:
                steps[i - CHUNKS].wait_recv()
            steps.append(remote(src, win.at[w, at], sw.at[i], rw.at[i], after))
            steps[i].start()

    relay(0)
    rows_in[head] = own[head]

    @pl.when((seq == 0) & (head < SINK_MOST))
    def _():
        piece[...] = own[0]

    for copy in loads:
        copy.wait()
    for raw, buf in ((q_raw, qbuf), (g_raw, gbuf)):
        for pair in range(KVH // 2):
            x = raw[:, 16 * pair : 16 * (pair + 1), :].astype(wide)
            for m in range(2):
                buf[2 * pair + m] = x[:, 8 * m : 8 * (m + 1)].reshape(COLUMNS, HD).astype(low)
    mine = lax.rem(head, 4)

    def piece_far(k):
        return remote(piece, pieces.at[mine], ss2.at[k], rs2.at[mine], {"head": lax.rem(head + 4 * k, N)})

    def piece_near(k):
        to = lax.rem(head + k, N)
        return remote(pieces.at[mine], pieces.at[mine], ss2.at[k], rs2.at[mine], {"head": to})

    lax.fori_loop(0, N, mark, 0)
    score_all(SINK_MOST, own)

    @pl.when((seq > 0) & (head < SINK_MOST))
    def _():
        remote(own.at[0], piece, ss1.at[0], rs1.at[0], {"seq": 0}).wait_recv()

    @pl.when(head < SINK_MOST)
    def _():
        for k in (2, 1, 3):
            piece_far(k).start()
        pieces[head] = piece[...]

    for copy in first:
        copy.wait_recv()
    for k in range(N):
        for c in range(CAP):
            slots_out[k, c] = rows_in[jnp.minimum(marks[k * CAP + c], N - 1)]
    second = exchange(slots_out, slots_in, s2, r2, seq, "seq")
    slots_in[seq] = slots_out[seq]

    relay(1)
    score_all(SINK_MOST + 1, win.at[0])
    slot_of = places()

    @pl.when((mine < SINK_MOST) & (head >= SINK_MOST))
    def _():
        remote(piece, pieces.at[mine], ss2.at[0], rs2.at[mine], {"head": mine}).wait_recv()

    @pl.when(mine < SINK_MOST)
    def _():
        for k in NEAR:
            piece_near(k).start()

    for copy in second:
        copy.wait_recv()
    for k in range(N):
        far_out[k] = slots_in[slot_of[k] >> 1, slot_of[k] & 1]
    third = exchange(far_out, kept, s3, r3, head, "head")
    kept[head] = far_out[head]

    for b in range(SINK_MOST):

        @pl.when(mine != b)
        def _():
            remote(piece, pieces.at[b], ss2.at[0], rs2.at[b], {"head": b}).wait_recv()

    spread = []
    for k in ORDER:
        to = lax.rem(seq + k, N)
        spread.append(remote(pieces, sink.at[seq], ss3.at[k], rs3.at[k], {"seq": to}))
        spread[-1].start()
    sink[seq] = pieces[...]

    relay(2)
    score_all(SINK_MOST + 2, win.at[1])

    for copy in steps[2 * CHUNKS :]:
        copy.wait_recv()
    score_all(SINK_MOST + 3, win.at[2])
    for copy in spread:
        copy.wait_recv()
    for b in range(SINK_MOST):

        def step(g, carry):
            k = sink[pl.ds(4 * g, 4), b, 0].reshape(BLK, HD)
            v = sink[pl.ds(4 * g, 4), b, 1].reshape(BLK, HD)
            score(g, b, k, v, ebuf.at[g, b], dbuf.at[g, b])
            return carry

        lax.fori_loop(0, KVH, step, 0)
    for copy in third:
        copy.wait_recv()


    def kept_step(g, carry):
        score(g, SLOTS - 1, part(kept, g, 0), part(kept, g, 1), efar, dfar)
        combine(g)

        def put(side, x):
            tkept[pl.ds(4 * g, 4), side] = x.astype(low)

        grad(g, SLOTS - 1, efar, dfar, put)
        return carry

    lax.fori_loop(0, KVH, kept_step, 0, unroll=True)
    first_back = exchange(tkept, rows, t1, v1, head, "head")
    rows[head] = tkept[head]
    rows[N] = jnp.zeros(PIECE, low)

    for b in range(SINK_MOST):

        def put_sink(at, side, x):
            tsink[at, b, side] = x.astype(low)

        grad_all(b, put_sink)
    spread_back = exchange(tsink, sink_in, ts3, vs3, seq, "seq")
    sink_in[seq] = tsink[seq]

    def put_hop(at, side, x):
        hop_out[0, at, side] = x.astype(low)

    grad_all(SLOTS - 2, put_hop)
    hops = []

    def hop(w):
        for c in range(CHUNKS):
            at = pl.ds(c * (N // CHUNKS), N // CHUNKS)
            i = w * CHUNKS + c
            if w > 0:
                hops[i - CHUNKS].wait_recv()
                hop_out[w, at] = (near[WIN_MOST - 1 - w, at] + hop_in[w - 1, at].astype(wide)).astype(low)
            hops.append(remote(hop_out.at[w, at], hop_in.at[w, at], tw.at[i], vw.at[i], before))
            hops[i].start()

    hop(0)
    lax.fori_loop(0, N * CAP, fill, 0)

    def put_near(n):
        def put(at, side, x):
            near[n, at, side] = x

        return put

    grad_all(SINK_MOST + 2, put_near(2))

    for copy in first_back:
        copy.wait_recv()
    for k in range(N):
        for c in range(CAP):
            back_out[k, c] = rows[fills[k * CAP + c]]
    second_back = exchange(back_out, back_in, t2, v2, seq, "seq")
    back_in[seq] = back_out[seq]

    for copy in spread_back:
        copy.wait_recv()
    for b in range(SINK_MOST):
        term = sink_in[0, b].astype(wide)
        for k in range(1, N):
            term = term + sink_in[k, b].astype(wide)
        shares[b] = term.astype(low)

    def share_near(b):
        r = lax.rem(head + 4 - b, 4)
        to = lax.rem(jnp.where(r == 3, head + 1, head + N - r), N)
        return remote(shares.at[b], shares_in.at[r], ts2.at[b], vs2.at[r], {"head": to})

    for b in range(SINK_MOST):

        @pl.when(mine != b)
        def _():
            share_near(b).start()

    hop(1)
    grad_all(SINK_MOST + 1, put_near(1))

    def share_far():
        k = 3 + head // 4
        return remote(share, shares_far.at[k - 4], ts2.at[3], vs2.at[k], {"head": mine})

    @pl.when(mine < SINK_MOST)
    def _():
        term = shares[mine].astype(wide)
        for k in range(1, 4):
            remote(shares.at[0], shares_in.at[k], ts2.at[3], vs2.at[k], {"head": mine}).wait_recv()
            term = term + shares_in[k].astype(wide)
        share[...] = term

    @pl.when((mine < SINK_MOST) & (head >= SINK_MOST))
    def _():
        share_far().start()

    lax.fori_loop(0, N * CAP, link, 0)
    lax.fori_loop(0, N, last, 0)
    run[...] = jnp.zeros(run.shape, wide)

    for copy in second_back:
        copy.wait_recv()
    for k in range(N):
        for c in range(CAP):
            i = k * CAP + c
            run[i] = back_in[k, c].astype(wide) + run[links[i]]
    for k in range(N):
        sums[k] = run[lasts[k]].astype(low)
    third_back = exchange(sums, sums_in, t3, v3, head, "head")
    sums_in[head] = sums[head]

    hop(2)

    grad_all(SINK_MOST, put_near(0))

    for g in range(KVH):
        turned = lax.dot_general(kbuf[g], sbuf[g], TN, preferred_element_type=wide)
        m = g % 2
        dqbuf[:, GROUP * m : GROUP * (m + 1), :] = (turned.T * scale).reshape(BLK, GROUP, HD)
        if m == 1:
            dq[:, GROUP * (g - 1) : GROUP * (g + 1), :] = dqbuf[...].astype(low)

    def whole_send():
        return remote(whole_out, whole.at[seq], ts1.at[0], vs1.at[seq], {"seq": 0})

    @pl.when(head < SINK_MOST)
    def _():
        term = share[...]
        for k in range(4, 7):
            remote(share, shares_far.at[k - 4], ts2.at[3], vs2.at[k], {"head": mine}).wait_recv()
            term = term + shares_far[k - 4]
        whole_out[...] = term

    @pl.when((head < SINK_MOST) & (seq > 0))
    def _():
        whole_send().start()

    for copy in hops[2 * CHUNKS :]:
        copy.wait_recv()
    total[...] = near[0] + hop_in[2].astype(wide)
    for copy in third_back:
        copy.wait_recv()
    total[...] = total[...] + sums_in[...].astype(wide)

    @pl.when((head < SINK_MOST) & (seq == 0))
    def _():
        whole[0] = whole_out[...]
        for k in range(1, N):
            remote(whole_out, whole.at[k], ts1.at[0], vs1.at[k], {"seq": k}).wait_recv()
        total[...] = total[...] + whole[...]

    for side, ref in ((0, dk), (1, dv)):
        heads = [total[4 * g : 4 * (g + 1), side].reshape(BLK, HD) for g in range(KVH)]
        ref[...] = jnp.stack(heads, axis=1).astype(low)


    for copy in steps + first + second + third + spread:
        copy.wait_send()
    for copy in hops + first_back + second_back + third_back + spread_back:
        copy.wait_send()

    @pl.when((seq == 0) & (head < SINK_MOST))
    def _():
        for k in range(1, N):
            sink_send(k).wait_send()

    @pl.when(head < SINK_MOST)
    def _():
        for k in (2, 1, 3):
            piece_far(k).wait_send()

    @pl.when(mine < SINK_MOST)
    def _():
        for k in NEAR:
            piece_near(k).wait_send()

    for b in range(SINK_MOST):

        @pl.when(mine != b)
        def _():
            share_near(b).wait_send()

    @pl.when((mine < SINK_MOST) & (head >= SINK_MOST))
    def _():
        share_far().wait_send()

    @pl.when((head < SINK_MOST) & (seq > 0))
    def _():
        whole_send().wait_send()


def attend(kept_blocks, sink_blocks, window_blocks, q, g, keys, values):
    low, wide = jnp.bfloat16, jnp.float32
    vmem = pl.BlockSpec(memory_space=pltpu.VMEM)
    smem = pl.BlockSpec(memory_space=pltpu.SMEM)
    hbm = pl.BlockSpec(memory_space=pl.ANY)
    dma = pltpu.SemaphoreType.DMA

    def lows(*lead):
        return pltpu.VMEM(lead + PIECE, low)

    def wides(*lead):
        return pltpu.VMEM(lead + PIECE, wide)

    raw = pltpu.VMEM((BLK, KVH * GROUP, HD), low)
    flat = pltpu.VMEM((KVH, COLUMNS, HD), low)
    rows = pltpu.VMEM((KVH, SLOTS, COLUMNS), wide)
    return pl.pallas_call(
        kernel,
        out_shape=(
            jax.ShapeDtypeStruct((BLK, KVH * GROUP, HD), low),
            jax.ShapeDtypeStruct((BLK, KVH, HD), low),
            jax.ShapeDtypeStruct((BLK, KVH, HD), low),
        ),
        in_specs=[smem, smem, smem, hbm, hbm, vmem, vmem],
        out_specs=(vmem, vmem, vmem),
        scratch_shapes=[
            lows(N),
            lows(N), lows(N, CAP), lows(N, CAP), lows(N), lows(), lows(SINK_MOST),
            lows(N, SINK_MOST), lows(WIN_MOST - 1, N), lows(N),
            lows(N, SINK_MOST), lows(N), wides(WIN_MOST - 1, N), lows(N + 1), lows(N, CAP), lows(N, CAP),
            wides(N * CAP + 1), lows(N), lows(N),
            lows(N, SINK_MOST), lows(SINK_MOST), lows(4), wides(3), wides(), wides(), wides(N),
            lows(WIN_MOST - 1, N), lows(WIN_MOST - 1, N), wides(N),
            raw, raw, flat, flat,
            pltpu.VMEM((KVH, SLOTS * BLK, HD), low),
            pltpu.VMEM((KVH, SLOTS - 1, BLK, COLUMNS), wide),
            pltpu.VMEM((KVH, SLOTS - 1, BLK, COLUMNS), wide),
            pltpu.VMEM((KVH, SLOTS * BLK, COLUMNS), low),
            pltpu.VMEM((BLK, COLUMNS), wide),
            pltpu.VMEM((BLK, COLUMNS), wide),
            rows, rows, rows, rows,
            pltpu.VMEM((KVH, 1, COLUMNS), wide),
            pltpu.VMEM((BLK, 2 * GROUP, HD), wide),
            pltpu.SMEM((N * CAP,), jnp.int32), pltpu.SMEM((N * CAP,), jnp.int32),
            pltpu.SMEM((N * CAP,), jnp.int32), pltpu.SMEM((N,), jnp.int32),
            dma((2,)),
            dma((3 * CHUNKS,)), dma((3 * CHUNKS,)), dma((N,)), dma((N,)), dma((N,)), dma((N,)), dma((N,)), dma((N,)),
            dma((N,)), dma((1,)), dma((N,)), dma((N,)), dma((N,)), dma((N,)),
            dma((3 * CHUNKS,)), dma((3 * CHUNKS,)), dma((N,)), dma((N,)), dma((N,)), dma((N,)), dma((N,)), dma((N,)),
            dma((1,)), dma((N,)), dma((4,)), dma((8,)), dma((N,)), dma((N,)),
        ],
        compiler_params=pltpu.CompilerParams(
            collective_id=0, has_side_effects=True, vmem_limit_bytes=VMEM_LIMIT
        ),
        name="attend",
    )(kept_blocks, sink_blocks, window_blocks, q, g, keys, values)


def body(queries, keys, values, out_grad, kept_blocks, sink_blocks, window_blocks):
    lists = kept_blocks.reshape(KVH, N * N)
    return attend(lists, sink_blocks, window_blocks, queries, out_grad, keys, values)


def solution(mesh):
    tokens = P(("dp", "seq", "head"), None, None)
    return jax.shard_map(
        body,
        mesh=mesh,
        in_specs=(tokens, tokens, tokens, tokens, P(), P(), P()),
        out_specs=(tokens, tokens, tokens),
        check_vma=False,
    )
```

time: 134 us -> 123 us (0.918)
  the two profiles are of different devices: /device:TPU:66 before, /device:TPU:24 now
where the time goes in v3:
time: 123 us; the launch traced here: 121 us
  Pallas kernels  115 us (93%)
  local copies, waits for them, and re-layouts  5.19 us (4%)
    pallas_call x1, Pallas kernels, attend(): pl.pallas_call(kernel, out_shape=(jax.ShapeDtypeStruct((BLK, KVH * GROUP,...  115 us
    unnamed x8, local copies, waits for them, and re-layouts  5.19 us

profile of v3, /device:TPU:24, one launch (start us, length us, event | category | flops | bytes accessed | tf_op | source)
XLA Modules:
  0.0 121.3 jit_solution(17722520500738181658)
XLA Ops:
  0.6 1.3 %copy.12 = s32[4,256,1]{1,0,2:T(4,128)} copy(s32[4,256,1]{1,2,0:T(1,128)} %param.11) | data formatting | bytes 8192
  1.9 115.4 %attend.1 = (bf16[128,32,128]{2,1,0:T(8,128)(2,1)}, bf16[128,4,128]{2,1,0:T(4,128)(2,1)}, bf16[128,4,128]{2,1,0:T(4,128)(2,1)}) custom-call(s32[4,256]{1,0:T(4,128)} %bitcast.3, s32[4]{0:T(128)} %sink_blocks.1, s32[4]{0:T(128)} %window_blocks.1, bf16[128,32,128]{2,1,0:T(8,128)(2,1)} %q_hbm.1, bf16[128,32,128]{2,1,0:T(8,128)(2,1)} %g_hbm.1, ...), custom_call_target="tpu_custom_call" | custom-call | tf_op jit(solution)/shard_map/attend/pallas_call | solution.py:539
  117.4 0.0 copy-start.1
  117.4 2.3 %copy.16 = bf16[128,32,128]{2,1,0:T(8,128)(2,1)} copy(bf16[128,32,128]{2,1,0:T(8,128)(2,1)} %get-tuple-element.6) | data formatting | bytes 2097152
  119.7 0.0 copy-done.1
  119.7 0.0 copy-start
  119.7 0.7 copy.17
  120.3 0.3 copy-done
  120.6 0.7 copy.18
Async XLA Ops:
  117.4 2.3 %copy-start.1 = (bf16[128,4,128]{2,1,0:T(4,128)(2,1)S(1)}, bf16[128,4,128]{2,1,0:T(4,128)(2,1)}, u32[]{:S(2)}) copy-start(bf16[128,4,128]{2,1,0:T(4,128)(2,1)} %get-tuple-element.7) | copy-start | bytes 393220
  119.7 1.0 copy-start

commit v4 on v3

--- a/solution.py
+++ b/solution.py
@@ -139,6 +139,27 @@
 
         lax.fori_loop(0, KVH, step, 0)
 
+    def score_sinks(g, carry):
+        k = jnp.concatenate([sink[pl.ds(4 * g, 4), b, 0].reshape(BLK, HD) for b in range(SINK_MOST)])
+        v = jnp.concatenate([sink[pl.ds(4 * g, 4), b, 1].reshape(BLK, HD) for b in range(SINK_MOST)])
+        kbuf[g, : SINK_MOST * BLK, :] = k
+        biases = [jnp.where(allowed(g, b), 0.0, -jnp.inf) for b in range(SINK_MOST)]
+        for i in range(COLUMNS // COLS):
+            here = slice(i * COLS, (i + 1) * COLS)
+            s = lax.dot_general(k, qbuf[g, here, :], NT, preferred_element_type=wide) * scale
+            d = lax.dot_general(v, gbuf[g, here, :], NT, preferred_element_type=wide)
+            for b in range(SINK_MOST):
+                rows_b = slice(b * BLK, (b + 1) * BLK)
+                t = s[rows_b] + biases[b]
+                top = jnp.maximum(jnp.max(t, axis=0, keepdims=True), LOWEST)
+                e = jnp.exp(t - top)
+                ebuf[g, b, :, here] = e
+                dbuf[g, b, :, here] = d[rows_b]
+                tops[g, b : b + 1, here] = top
+                norms[g, b : b + 1, here] = jnp.sum(e, axis=0, keepdims=True)
+                deltas[g, b : b + 1, here] = jnp.sum(e * d[rows_b], axis=0, keepdims=True)
+        return carry
+
     def combine(g):
         t = tops[g]
         w = jnp.exp(t - jnp.max(t, axis=0, keepdims=True))
@@ -153,6 +174,22 @@
         put(0, (lax.dot_general(ds, qbuf[g], NN, preferred_element_type=wide) * scale).reshape(4, ROWS, HD))
         dv = lax.dot_general(p.astype(low), gbuf[g], NN, preferred_element_type=wide)
         put(1, dv.reshape(4, ROWS, HD))
+
+    def grad_sinks(g, carry):
+        terms = []
+        for b in range(SINK_MOST):
+            p = ebuf[g, b] * factors[g, b : b + 1, :]
+            terms.append((p.astype(low), (p * (dbuf[g, b] - centre[g])).astype(low)))
+        p = jnp.concatenate([t[0] for t in terms])
+        ds = jnp.concatenate([t[1] for t in terms])
+        sbuf[g, : SINK_MOST * BLK, :] = ds
+        dk = lax.dot_general(ds, qbuf[g], NN, preferred_element_type=wide) * scale
+        dv = lax.dot_general(p, gbuf[g], NN, preferred_element_type=wide)
+        for b in range(SINK_MOST):
+            for side, x in ((0, dk), (1, dv)):
+                part_b = x[b * BLK : (b + 1) * BLK].reshape(4, ROWS, HD)
+                tsink[pl.ds(4 * g, 4), b, side] = part_b.astype(low)
+        return carry
 
     def grad_all(slot, put):
         def step(g, carry):
@@ -253,9 +290,6 @@
         to = lax.rem(head + k, N)
         return remote(pieces.at[mine], pieces.at[mine], ss2.at[k], rs2.at[mine], {"head": to})
 
-    lax.fori_loop(0, N, mark, 0)
-    score_all(SINK_MOST, own)
-
     @pl.when((seq > 0) & (head < SINK_MOST))
     def _():
         remote(own.at[0], piece, ss1.at[0], rs1.at[0], {"seq": 0}).wait_recv()
@@ -265,6 +299,9 @@
         for k in (2, 1, 3):
             piece_far(k).start()
         pieces[head] = piece[...]
+
+    lax.fori_loop(0, N, mark, 0)
+    score_all(SINK_MOST, own)
 
     for copy in first:
         copy.wait_recv()
@@ -274,25 +311,18 @@
     second = exchange(slots_out, slots_in, s2, r2, seq, "seq")
     slots_in[seq] = slots_out[seq]
 
+    @pl.when((mine < SINK_MOST) & (head >= SINK_MOST))
+    def _():
+        remote(piece, pieces.at[mine], ss2.at[0], rs2.at[mine], {"head": mine}).wait_recv()
+
+    @pl.when(mine < SINK_MOST)
+    def _():
+        for k in NEAR:
+            piece_near(k).start()
+
     relay(1)
     score_all(SINK_MOST + 1, win.at[0])
     slot_of = places()
-
-    @pl.when((mine < SINK_MOST) & (head >= SINK_MOST))
-    def _():
-        remote(piece, pieces.at[mine], ss2.at[0], rs2.at[mine], {"head": mine}).wait_recv()
-
-    @pl.when(mine < SINK_MOST)
-    def _():
-        for k in NEAR:
-            piece_near(k).start()
-
-    for copy in second:
-        copy.wait_recv()
-    for k in range(N):
-        far_out[k] = slots_in[slot_of[k] >> 1, slot_of[k] & 1]
-    third = exchange(far_out, kept, s3, r3, head, "head")
-    kept[head] = far_out[head]
 
     for b in range(SINK_MOST):
 
@@ -307,23 +337,22 @@
         spread[-1].start()
     sink[seq] = pieces[...]
 
+    for copy in second:
+        copy.wait_recv()
+    for k in range(N):
+        far_out[k] = slots_in[slot_of[k] >> 1, slot_of[k] & 1]
+    third = exchange(far_out, kept, s3, r3, head, "head")
+    kept[head] = far_out[head]
+
     relay(2)
     score_all(SINK_MOST + 2, win.at[1])
 
+    for copy in spread:
+        copy.wait_recv()
+    lax.fori_loop(0, KVH, score_sinks, 0)
     for copy in steps[2 * CHUNKS :]:
         copy.wait_recv()
     score_all(SINK_MOST + 3, win.at[2])
-    for copy in spread:
-        copy.wait_recv()
-    for b in range(SINK_MOST):
-
-        def step(g, carry):
-            k = sink[pl.ds(4 * g, 4), b, 0].reshape(BLK, HD)
-            v = sink[pl.ds(4 * g, 4), b, 1].reshape(BLK, HD)
-            score(g, b, k, v, ebuf.at[g, b], dbuf.at[g, b])
-            return carry
-
-        lax.fori_loop(0, KVH, step, 0)
     for copy in third:
         copy.wait_recv()
 
@@ -343,12 +372,7 @@
     rows[head] = tkept[head]
     rows[N] = jnp.zeros(PIECE, low)
 
-    for b in range(SINK_MOST):
-
-        def put_sink(at, side, x):
-            tsink[at, b, side] = x.astype(low)
-
-        grad_all(b, put_sink)
+    lax.fori_loop(0, KVH, grad_sinks, 0)
     spread_back = exchange(tsink, sink_in, ts3, vs3, seq, "seq")
     sink_in[seq] = tsink[seq]
 

time: 123 us -> 119 us (0.967); the launches traced: 121 us -> 119 us
  Pallas kernels: 115 us -> 113 us
    pallas_call x1, Pallas kernels: 115 us -> 113 us  [attend(): pl.pallas_call(kernel, out_shape=(jax.ShapeDtypeStruct((BLK, KVH * GROUP,...]
where the time goes in v4:
time: 119 us
  Pallas kernels  113 us (95%)
  local copies, waits for them, and re-layouts  5.19 us (4%)
    pallas_call x1, Pallas kernels, attend(): pl.pallas_call(kernel, out_shape=(jax.ShapeDtypeStruct((BLK, KVH * GROUP,...  113 us
    unnamed x8, local copies, waits for them, and re-layouts  5.19 us

profile of v4, /device:TPU:24, one launch (start us, length us, event | category | flops | bytes accessed | tf_op | source)
XLA Modules:
  0.0 119.2 jit_solution(11236912569928865097)
XLA Ops:
  0.6 1.3 %copy.12 = s32[4,256,1]{1,0,2:T(4,128)} copy(s32[4,256,1]{1,2,0:T(1,128)} %param.11) | data formatting | bytes 8192
  1.9 113.4 %attend.1 = (bf16[128,32,128]{2,1,0:T(8,128)(2,1)}, bf16[128,4,128]{2,1,0:T(4,128)(2,1)}, bf16[128,4,128]{2,1,0:T(4,128)(2,1)}) custom-call(s32[4,256]{1,0:T(4,128)} %bitcast.3, s32[4]{0:T(128)} %sink_blocks.1, s32[4]{0:T(128)} %window_blocks.1, bf16[128,32,128]{2,1,0:T(8,128)(2,1)} %q_hbm.1, bf16[128,32,128]{2,1,0:T(8,128)(2,1)} %g_hbm.1, ...), custom_call_target="tpu_custom_call" | custom-call | tf_op jit(solution)/shard_map/attend/pallas_call | solution.py:563
  115.3 0.0 copy-start.1
  115.3 2.3 %copy.16 = bf16[128,32,128]{2,1,0:T(8,128)(2,1)} copy(bf16[128,32,128]{2,1,0:T(8,128)(2,1)} %get-tuple-element.6) | data formatting | bytes 2097152
  117.6 0.0 copy-done.1
  117.6 0.0 copy-start
  117.6 0.7 copy.17
  118.3 0.3 copy-done
  118.6 0.7 copy.18
Async XLA Ops:
  115.3 2.3 %copy-start.1 = (bf16[128,4,128]{2,1,0:T(4,128)(2,1)S(1)}, bf16[128,4,128]{2,1,0:T(4,128)(2,1)}, u32[]{:S(2)}) copy-start(bf16[128,4,128]{2,1,0:T(4,128)(2,1)} %get-tuple-element.7) | copy-start | bytes 393220
  117.6 1.0 copy-start

commit v5 on v4

--- a/solution.py
+++ b/solution.py
@@ -50,7 +50,10 @@
     pl.semaphore_wait(barrier, 2 * (N - 1) + 2)
 
 
-ORDER = [8] + [k for i in range(1, 8) for k in (i, N - i)]
+ORDERS = {
+    "head": [8] + [k for i in range(7, 0, -1) for k in (i, N - i)],
+    "seq": [10, 6, 14, 9, 11, 2, 8, 5, 7, 13, 15, 1, 3, 4, 12],
+}
 COLS = 256
 CHUNKS = 2
 NEAR = (2, 1, N - 1)
@@ -63,7 +66,7 @@
 
 def exchange(src, dst, send, recv, me, axis):
     copies = []
-    for k in ORDER:
+    for k in ORDERS[axis]:
         to = lax.rem(me + k, N)
         copies.append(remote(src.at[to], dst.at[me], send.at[k], recv.at[k], {axis: to}))
         copies[-1].start()
@@ -331,7 +334,7 @@
             remote(piece, pieces.at[b], ss2.at[0], rs2.at[b], {"head": b}).wait_recv()
 
     spread = []
-    for k in ORDER:
+    for k in ORDERS["seq"]:
         to = lax.rem(seq + k, N)
         spread.append(remote(pieces, sink.at[seq], ss3.at[k], rs3.at[k], {"seq": to}))
         spread[-1].start()

time: 119 us -> 122 us (1.025)
  the two profiles are of different devices: /device:TPU:24 before, /device:TPU:32 now
where the time goes in v5:
time: 122 us
  Pallas kernels  116 us (95%)
  local copies, waits for them, and re-layouts  5.19 us (4%)
    pallas_call x1, Pallas kernels, attend(): pl.pallas_call(kernel, out_shape=(jax.ShapeDtypeStruct((BLK, KVH * GROUP,...  116 us
    unnamed x8, local copies, waits for them, and re-layouts  5.19 us

profile of v5, /device:TPU:32, one launch (start us, length us, event | category | flops | bytes accessed | tf_op | source)
XLA Modules:
  0.0 121.7 jit_solution(16848468451786111629)
XLA Ops:
  0.6 1.3 %copy.12 = s32[4,256,1]{1,0,2:T(4,128)} copy(s32[4,256,1]{1,2,0:T(1,128)} %param.11) | data formatting | bytes 8192
  1.9 115.9 %attend.1 = (bf16[128,32,128]{2,1,0:T(8,128)(2,1)}, bf16[128,4,128]{2,1,0:T(4,128)(2,1)}, bf16[128,4,128]{2,1,0:T(4,128)(2,1)}) custom-call(s32[4,256]{1,0:T(4,128)} %bitcast.3, s32[4]{0:T(128)} %sink_blocks.1, s32[4]{0:T(128)} %window_blocks.1, bf16[128,32,128]{2,1,0:T(8,128)(2,1)} %q_hbm.1, bf16[128,32,128]{2,1,0:T(8,128)(2,1)} %g_hbm.1, ...), custom_call_target="tpu_custom_call" | custom-call | tf_op jit(solution)/shard_map/attend/pallas_call | solution.py:566
  117.8 0.0 copy-start.1
  117.8 2.3 %copy.16 = bf16[128,32,128]{2,1,0:T(8,128)(2,1)} copy(bf16[128,32,128]{2,1,0:T(8,128)(2,1)} %get-tuple-element.6) | data formatting | bytes 2097152
  120.1 0.0 copy-done.1
  120.1 0.0 copy-start
  120.1 0.7 copy.17
  120.8 0.3 copy-done
  121.1 0.7 copy.18
Async XLA Ops:
  117.8 2.3 %copy-start.1 = (bf16[128,4,128]{2,1,0:T(4,128)(2,1)S(1)}, bf16[128,4,128]{2,1,0:T(4,128)(2,1)}, u32[]{:S(2)}) copy-start(bf16[128,4,128]{2,1,0:T(4,128)(2,1)} %get-tuple-element.7) | copy-start | bytes 393220
  120.1 1.0 copy-start

commit v6 on v4

--- a/solution.py
+++ b/solution.py
@@ -137,7 +137,7 @@
             score(g, slot, part(ref, g, 0), part(ref, g, 1), ebuf.at[g, slot], dbuf.at[g, slot])
             return carry
 
-        lax.fori_loop(0, KVH, step, 0)
+        lax.fori_loop(0, KVH, step, 0, unroll=2)
 
     def score_sinks(g, carry):
         k = jnp.concatenate([sink[pl.ds(4 * g, 4), b, 0].reshape(BLK, HD) for b in range(SINK_MOST)])
@@ -196,7 +196,7 @@
             grad(g, slot, ebuf.at[g, slot], dbuf.at[g, slot], lambda side, x: put(pl.ds(4 * g, 4), side, x))
             return carry
 
-        lax.fori_loop(0, KVH, step, 0)
+        lax.fori_loop(0, KVH, step, 0, unroll=2)
 
 
     group = head // 4
@@ -349,7 +349,7 @@
 
     for copy in spread:
         copy.wait_recv()
-    lax.fori_loop(0, KVH, score_sinks, 0)
+    lax.fori_loop(0, KVH, score_sinks, 0, unroll=2)
     for copy in steps[2 * CHUNKS :]:
         copy.wait_recv()
     score_all(SINK_MOST + 3, win.at[2])
@@ -372,7 +372,7 @@
     rows[head] = tkept[head]
     rows[N] = jnp.zeros(PIECE, low)
 
-    lax.fori_loop(0, KVH, grad_sinks, 0)
+    lax.fori_loop(0, KVH, grad_sinks, 0, unroll=2)
     spread_back = exchange(tsink, sink_in, ts3, vs3, seq, "seq")
     sink_in[seq] = tsink[seq]
 

time: 119 us -> 118 us (level)
    pallas_call x1, Pallas kernels: 113 us -> 112 us  [attend(): pl.pallas_call(kernel, out_shape=(jax.ShapeDtypeStruct((BLK, KVH * GROUP,...]
where the time goes in v6:
time: 118 us; the launch traced here: 117 us
  Pallas kernels  112 us (95%)
  local copies, waits for them, and re-layouts  5.19 us (4%)
    pallas_call x1, Pallas kernels, attend(): pl.pallas_call(kernel, out_shape=(jax.ShapeDtypeStruct((BLK, KVH * GROUP,...  112 us
    unnamed x8, local copies, waits for them, and re-layouts  5.19 us

profile of v6, /device:TPU:24, one launch (start us, length us, event | category | flops | bytes accessed | tf_op | source)
XLA Modules:
  0.0 117.3 jit_solution(1623820252610391222)
XLA Ops:
  0.6 1.3 %copy.12 = s32[4,256,1]{1,0,2:T(4,128)} copy(s32[4,256,1]{1,2,0:T(1,128)} %param.11) | data formatting | bytes 8192
  1.9 111.5 %attend.1 = (bf16[128,32,128]{2,1,0:T(8,128)(2,1)}, bf16[128,4,128]{2,1,0:T(4,128)(2,1)}, bf16[128,4,128]{2,1,0:T(4,128)(2,1)}) custom-call(s32[4,256]{1,0:T(4,128)} %bitcast.3, s32[4]{0:T(128)} %sink_blocks.1, s32[4]{0:T(128)} %window_blocks.1, bf16[128,32,128]{2,1,0:T(8,128)(2,1)} %q_hbm.1, bf16[128,32,128]{2,1,0:T(8,128)(2,1)} %g_hbm.1, ...), custom_call_target="tpu_custom_call" | custom-call | tf_op jit(solution)/shard_map/attend/pallas_call | solution.py:563
  113.4 0.0 copy-start.1
  113.4 2.3 %copy.16 = bf16[128,32,128]{2,1,0:T(8,128)(2,1)} copy(bf16[128,32,128]{2,1,0:T(8,128)(2,1)} %get-tuple-element.6) | data formatting | bytes 2097152
  115.7 0.0 copy-done.1
  115.7 0.0 copy-start
  115.7 0.7 copy.17
  116.4 0.3 copy-done
  116.7 0.7 copy.18
Async XLA Ops:
  113.4 2.3 %copy-start.1 = (bf16[128,4,128]{2,1,0:T(4,128)(2,1)S(1)}, bf16[128,4,128]{2,1,0:T(4,128)(2,1)}, u32[]{:S(2)}) copy-start(bf16[128,4,128]{2,1,0:T(4,128)(2,1)} %get-tuple-element.7) | copy-start | bytes 393220
  115.7 1.0 copy-start
